TPU v7x, 256 devices: a whole 4x4x8 slice. The times are simulated.
256 devices in a mesh: grp: 2 (over z_hi), lat: 128 (over x, y, z_lo, core).
Axes of the slice: x: 4, y: 4, z: 8 (z_hi: 2, z_lo: 4; z = z_hi * 4 + z_lo), core: 2. Of those that a mesh axis runs over, the one named last changes fastest.
Arguments:
- fields: bfloat16 [2, 256, 128, 384], P('grp', 'lat'), may hold values from -6 to 6
- cotangent: bfloat16 [2, 256, 128, 384], P('grp', 'lat'), may hold values from -6 to 6
- ocean_kernels: bfloat16 [2, 3, 3, 192, 192], replicated, may hold values from -0.15625 to 0.15625
- atmos_kernels: bfloat16 [2, 3, 3, 384, 384], replicated, may hold values from -0.109375 to 0.109375
- ocean_surface: bfloat16 [192, 4], replicated, may hold values from -0.4375 to 0.4375
- ocean_coupling: bfloat16 [4, 192], replicated, may hold values from -3 to 3
- atmos_flux: bfloat16 [384, 4], replicated, may hold values from -0.3125 to 0.3125
- atmos_coupling: bfloat16 [4, 384], replicated, may hold values from -3 to 3
- row_map: int32 [256], P('lat'), may hold values from 0 to 255, as said below
- wet_mask: int32 [256, 256], P('lat'), may hold values 0 or 1
Outputs:
- next_fields: bfloat16 [2, 256, 128, 384], P('grp', 'lat')
- field_grads: bfloat16 [2, 256, 128, 384], P('grp', 'lat')
- ocean_kernel_grad: float32 [663552], P(('grp', 'lat'))
- atmos_kernel_grad: float32 [2654208], P(('grp', 'lat'))
Inputs may be any that keep to these rules, and one draw needn't show every extreme that they name: row_map never falls, keeps each ocean row in its own band of 2 rows, and maps the first and last row of every band to that band's first and last row.
All inputs are finite; a program needn't handle non-finite values. No bound on the sum of `wet_mask` on one device may be relied on, other than what follows from the above.
Results may differ from a plain program's by a relative error of at most 0.0065.
Values may be sent and summed in bfloat16 or wider, within the bound.
A program may use at most 128 MiB of HBM per device.

v0:
```python
import math

import jax
import jax.numpy as jnp
from jax import lax
from jax.experimental import pallas as pl
from jax.experimental.pallas import tpu as pltpu
from jax.sharding import PartitionSpec as P

MESH = pl.DeviceIdType.MESH
F32 = jnp.float32
BF16 = jnp.bfloat16
GELU_SCALE = 0.7978845608028654
GELU_CUBIC = 0.044715
CH = 384
COLS = 128
WIN = 224
NSEM = 64


def nt_dot(a, b):
    return lax.dot_general(a, b, (((1,), (1,)), ((), ())), preferred_element_type=F32)


def tn_dot(a, b):
    return lax.dot_general(a, b, (((0,), (0,)), ((), ())), preferred_element_type=F32)


def mm(a, b):
    return jnp.dot(a, b, preferred_element_type=F32)


def split_pair(values):
    high = values.astype(BF16).astype(F32)
    return jnp.concatenate([high, values - high], axis=0).astype(BF16)


def body(
    x_ref, g_ref, ak_ref, ok_ref, m_ref, c_ref, wm_ref,
    next_ref, fgrad_ref, grads_ref,
    w, okv, xp, gp, hp, fp, up, gcat, ucat, hcat, fcat,
    wmp, trs, trp, tr2s, tr2r, first, bh, ig,
    s_a, r_a, s_b, r_b, b4, b4s, at, at2,
    part, rec1, rec2, part2, rec3, rec4, dsum, zrec, esum, fin, out,
    wsem, ssem, rsem,
):
    g = lax.axis_index("grp")
    lat = lax.axis_index("lat")
    core = lat % 2
    z = (lat // 2) % 4
    y = (lat // 8) % 4
    x = lat // 32

    def spot(xx, yy, zz, cc):
        return xx * 32 + yy * 8 + zz * 2 + cc

    dn = (lat + 1) % 128
    up_lat = (lat + 127) % 128
    x_plus, x_minus = spot((x + 1) % 4, y, z, core), spot((x + 3) % 4, y, z, core)
    y_plus, y_minus = spot(x, (y + 1) % 4, z, core), spot(x, (y + 3) % 4, z, core)
    z_other = [spot(x, y, (z + k) % 4, core) for k in (1, 2, 3)]
    mate = lat + 1 - 2 * core
    has_top = jnp.where(lat > 0, 1.0, 0.0).astype(F32)
    has_low = jnp.where(lat < 127, 1.0, 0.0).astype(F32)
    edge = [has_top, None, None, has_low]

    atmos_copy = pltpu.make_async_copy(ak_ref, w, wsem.at[0])
    ocean_copy = pltpu.make_async_copy(ok_ref, okv, wsem.at[1])

    @pl.when(g == 1)
    def _():
        atmos_copy.start()

    @pl.when(g == 0)
    def _():
        ocean_copy.start()

    barrier = pltpu.get_barrier_semaphore()
    partners = [(g, dn), (g, up_lat), (1 - g, lat), (1 - g, dn), (1 - g, up_lat)]
    partners += [(g, other) for other in (x_plus, x_minus, y_plus, y_minus, *z_other)]
    for device in partners:
        pl.semaphore_signal(barrier, inc=1, device_id=device, device_id_type=MESH)
    pl.semaphore_wait(barrier, len(partners))

    used = []

    def send(src, dst, device):
        index = len(used)
        copy = pltpu.make_async_remote_copy(
            src_ref=src, dst_ref=dst, send_sem=ssem.at[index], recv_sem=rsem.at[index],
            device_id=device, device_id_type=MESH,
        )
        copy.start()
        used.append(copy)
        return copy

    g_low = send(g_ref.at[1], gp.at[0], (g, dn))
    g_top = send(g_ref.at[0], gp.at[3], (g, up_lat))
    x_low = send(x_ref.at[1], xp.at[0], (g, dn))
    x_top = send(x_ref.at[0], xp.at[3], (g, up_lat))
    m_low = send(wm_ref.at[1, 0], wmp.at[0], (g, dn))
    m_top = send(wm_ref.at[0, 0], wmp.at[3], (g, up_lat))

    for row in range(2):
        shown = nt_dot(m_ref[...], x_ref[row])[0:8] * wm_ref[row, 0]
        trs[row] = (shown + pltpu.roll(shown, 4, 0)) * wm_ref[row, 1]
    t_mid = send(trs, trp.at[pl.ds(1, 2)], (1 - g, lat))
    t_low = send(trs.at[1], trp.at[0], (1 - g, dn))
    t_top = send(trs.at[0], trp.at[3], (1 - g, up_lat))

    column = lax.broadcasted_iota(jnp.int32, (COLS, CH), 0)

    def put_cat(dst, index, values):
        dst[index, :, CH:2 * CH] = values.astype(BF16)
        dst[index, :, 0:CH] = jnp.where(column > 0, pltpu.roll(values, 1, 0), 0.0).astype(BF16)
        dst[index, :, 2 * CH:3 * CH] = jnp.where(
            column < COLS - 1, pltpu.roll(values, COLS - 1, 0), 0.0
        ).astype(BF16)

    def conv(cat, layer):
        total = None
        for p in range(3):
            term = mm(cat[p:p + 2].reshape(2 * COLS, 3 * CH), w[layer, p])
            total = term if total is None else total + term
        return total

    def conv_back(cat, layer):
        total = None
        for p in range(3):
            for q in range(3):
                rows = cat[p:p + 2, :, q * CH:(q + 1) * CH].reshape(2 * COLS, CH)
                term = nt_dot(rows, w[layer, 2 - p, (2 - q) * CH:(3 - q) * CH, :])
                total = term if total is None else total + term
        return total

    @pl.when(g == 0)
    def _():
        ocean_copy.wait()
        half = CH // 2
        row_id = lax.broadcasted_iota(jnp.int32, (half, CH), 0)
        lane_id = lax.broadcasted_iota(jnp.int32, (half, CH), 1)
        lower = jnp.where(row_id == lane_id, 1.0, 0.0).astype(BF16)
        upper = jnp.where(row_id + half == lane_id, 1.0, 0.0).astype(BF16)
        zero = jnp.zeros((half, CH), BF16)
        for layer in range(2):
            for p in range(3):
                taps = [okv[layer, p, half * q:half * (q + 1), :] for q in range(3)]
                low = [mm(tap, lower) for tap in taps]
                high = [mm(tap, upper) for tap in taps]
                blocks = [low[0], low[1] + high[0], low[2] + high[1], high[2]]
                w[layer, p, 0:half, :] = zero
                w[layer, p, 5 * half:6 * half, :] = zero
                for index, block in enumerate(blocks):
                    w[layer, p, (index + 1) * half:(index + 2) * half, :] = block.astype(BF16)

    @pl.when(g == 1)
    def _():
        atmos_copy.wait()

    for row in range(2):
        put_cat(gcat, row + 1, g_ref[row].astype(F32))
    g_low.wait_recv()
    g_top.wait_recv()
    put_cat(gcat, 0, gp[0].astype(F32) * has_top)
    put_cat(gcat, 3, gp[3].astype(F32) * has_low)
    bh[...] = conv_back(gcat, 1)

    for copy in (x_low, x_top, m_low, m_top, t_mid, t_low, t_top):
        copy.wait_recv()
    for index in range(4):
        values = xp[index] if index in (0, 3) else x_ref[index - 1]
        mask = wmp[index] if index in (0, 3) else wm_ref[index - 1, 0]
        term = tn_dot(split_pair(mask * trp[index]), c_ref[...])
        total = (values.astype(F32) + term).astype(BF16).astype(F32)
        if edge[index] is not None:
            total = total * edge[index]
        up[index] = total.astype(BF16)
        put_cat(ucat, index, total)
    zed = conv(ucat, 0)
    tangent = jnp.tanh(GELU_SCALE * (zed + GELU_CUBIC * zed * zed * zed))
    hidden = (0.5 * zed * (1.0 + tangent)).astype(BF16).reshape(2, COLS, CH)
    slope = 0.5 * (1.0 + tangent) + 0.5 * zed * (1.0 - tangent * tangent) * GELU_SCALE * (
        1.0 + 3.0 * GELU_CUBIC * zed * zed
    )
    first_grad = (bh[...] * slope).astype(BF16).reshape(2, COLS, CH)
    hp[1:3] = hidden
    fp[1:3] = first_grad
    h_low = send(hp.at[2], hp.at[0], (g, dn))
    h_top = send(hp.at[1], hp.at[3], (g, up_lat))
    f_low = send(fp.at[2], fp.at[0], (g, dn))
    f_top = send(fp.at[1], fp.at[3], (g, up_lat))

    @pl.when(core == 0)
    def _():
        s_b[...] = g_ref[...]

    @pl.when(core == 1)
    def _():
        s_b[...] = fp[1:3]

    pair_b = send(s_b, r_b, (g, mate))
    for row in (1, 2):
        put_cat(hcat, row, hp[row].astype(F32))
        put_cat(fcat, row, fp[row].astype(F32))
    h_low.wait_recv()
    h_top.wait_recv()
    put_cat(hcat, 0, hp[0].astype(F32) * has_top)
    put_cat(hcat, 3, hp[3].astype(F32) * has_low)

    @pl.when(core == 0)
    def _():
        s_a[...] = hcat[0:2, :, CH:2 * CH]

    @pl.when(core == 1)
    def _():
        s_a[...] = up[2:4]

    pair_a = send(s_a, r_a, (g, mate))
    next_ref[...] = (up[1:3].astype(F32) + conv(hcat, 1).reshape(2, COLS, CH)).astype(BF16)
    pair_b.wait_recv()
    pair_a.wait_recv()

    @pl.when(core == 0)
    def _():
        b4[0:256] = fp[1:3].reshape(256, CH)
        b4[256:512] = r_b[...].reshape(256, CH)

    @pl.when(core == 1)
    def _():
        b4[0:256] = r_b[...].reshape(256, CH)
        b4[256:512] = g_ref[...].reshape(256, CH)

    put_cat(gcat, 0, r_a[0].astype(F32))
    put_cat(gcat, 1, r_a[1].astype(F32))

    def put_turned(index, source):
        turned = source.astype(F32).T.astype(BF16)

        @pl.when(g == 1)
        def _():
            for p in range(3):
                k = index - p
                if 0 <= k <= 3:
                    at[3 * CH * p:3 * CH * (p + 1), k * COLS:(k + 1) * COLS] = turned

        @pl.when(g == 0)
        def _():
            for p in range(3):
                k = index - p
                if 0 <= k <= 3:
                    at[576 * p:576 * (p + 1), k * COLS:(k + 1) * COLS] = turned[192:768]
                    at2[576 * p:576 * (p + 1), k * COLS:(k + 1) * COLS] = turned[384:960]

    @pl.when(core == 0)
    def _():
        for index in range(6):
            put_turned(index, ucat[index] if index < 4 else gcat[index - 4])

    @pl.when(core == 1)
    def _():
        for index in range(6):
            put_turned(index, gcat[index] if index < 2 else hcat[index - 2])

    def lane2(xq, yq):
        return xq + core * (yq - xq), yq + core * (xq - yq)

    @pl.when(g == 1)
    def _():
        def window(index, carry):
            xq, yq = index // 4, index % 4
            start = pl.multiple_of(index * 216 - 8 * (index % 2), 16)
            made = mm(at[pl.ds(start, WIN), :], b4[...]).astype(BF16)
            a2, b2 = lane2(xq, yq)
            part[0, xq, pl.ds(pl.multiple_of(yq * WIN, 16), WIN), :] = made[:, 0:128]
            part[1, yq, pl.ds(pl.multiple_of(xq * WIN, 16), WIN), :] = made[:, 128:256]
            part[2, a2, pl.ds(pl.multiple_of(b2 * WIN, 16), WIN), :] = made[:, 256:384]
            return carry

        lax.fori_loop(0, 16, window, 0)

    @pl.when(g == 0)
    def _():
        row_id = lax.broadcasted_iota(jnp.int32, (CH, 256), 0)
        lane_id = lax.broadcasted_iota(jnp.int32, (CH, 256), 1)
        swap = jnp.where(row_id == lane_id + 192, 1.0, 0.0).astype(BF16)
        b4s[...] = mm(b4[...], swap).astype(BF16)

        def window(index, carry):
            xq, yq = index // 4, index % 4
            start = pl.multiple_of(index * 108 - (12 * index) % 16, 16)
            made = mm(at[pl.ds(start, 128), :], b4[:, 0:256])
            made = (made + mm(at2[pl.ds(start, 128), :], b4s[...])).astype(BF16)
            part[0, xq, pl.ds(pl.multiple_of(yq * WIN, 16), 128), :] = made[:, 0:128]
            part[1, yq, pl.ds(pl.multiple_of(xq * WIN, 16), 128), :] = made[:, 128:256]
            return carry

        lax.fori_loop(0, 16, window, 0)

    ids_x, ids_y = (x, x_plus, x_minus), (y, y_plus, y_minus)
    mixed_a = tuple(a + core * (b - a) for a, b in zip(ids_x, ids_y))
    mixed_b = tuple(b + core * (a - b) for a, b in zip(ids_x, ids_y))
    orders = [(ids_x, ids_y), (ids_y, ids_x), (mixed_a, mixed_b)]

    def ring_start(lane, ids, source, near, far, rows):
        me, plus, minus = ids
        half = rows // 2
        low, high = pl.ds(0, half), pl.ds(half, half)
        ahead, behind, across = (me + 1) % 4, (me + 3) % 4, (me + 2) % 4
        one_p = send(source.at[lane, across, low], near.at[lane, 0], (g, plus))
        one_m = send(source.at[lane, across, high], near.at[lane, 1], (g, minus))
        two_p = send(source.at[lane, ahead, high], far.at[lane, 0, high], (g, plus))
        two_m = send(source.at[lane, behind, low], far.at[lane, 1, low], (g, minus))
        return one_p, one_m, two_p, two_m

    def ring_relay(lane, ids, source, near, far, rows, early):
        me, plus, minus = ids
        half = rows // 2
        low, high = pl.ds(0, half), pl.ds(half, half)
        ahead, behind = (me + 1) % 4, (me + 3) % 4
        early[0].wait_recv()
        source[lane, ahead, low, :] = (
            source[lane, ahead, low, :].astype(F32) + near[lane, 0].astype(F32)
        ).astype(BF16)
        three_p = send(source.at[lane, ahead, low], far.at[lane, 0, low], (g, plus))
        early[1].wait_recv()
        source[lane, behind, high, :] = (
            source[lane, behind, high, :].astype(F32) + near[lane, 1].astype(F32)
        ).astype(BF16)
        three_m = send(source.at[lane, behind, high], far.at[lane, 1, high], (g, minus))
        return early[2], early[3], three_p, three_m

    def ring_sum(lane, ids, source, far, late):
        for copy in late:
            copy.wait_recv()
        me = ids[0]
        return (
            source[lane, me].astype(F32) + far[lane, 0].astype(F32) + far[lane, 1].astype(F32)
        ).astype(BF16)

    begun = [ring_start(k, orders[k][0], part, rec1, rec2, 4 * WIN) for k in range(3)]

    f_low.wait_recv()
    f_top.wait_recv()
    put_cat(fcat, 0, fp[0].astype(F32) * has_top)
    put_cat(fcat, 3, fp[3].astype(F32) * has_low)
    ig[...] = g_ref[...].reshape(2 * COLS, CH).astype(F32) + conv_back(fcat, 0)

    begun = [ring_relay(k, orders[k][0], part, rec1, rec2, 4 * WIN, begun[k]) for k in range(3)]

    for row in range(2):
        grad = ig[row * COLS:(row + 1) * COLS, :]
        high = grad.astype(BF16)
        low = (grad - high.astype(F32)).astype(BF16)
        shown = (nt_dot(c_ref[...], high) + nt_dot(c_ref[...], low))[0:8] * wm_ref[row, 0]
        tr2s[row] = shown + pltpu.roll(shown, 4, 0)
    back = send(tr2s, tr2r, (1 - g, lat))

    begun2 = []
    for k in range(3):
        part2[k] = ring_sum(k, orders[k][0], part, rec2, begun[k]).reshape(4, WIN, 128)
        begun2.append(ring_start(k, orders[k][1], part2, rec3, rec4, WIN))

    back.wait_recv()
    for row in range(2):
        left = split_pair(wm_ref[row, 0] * wm_ref[row, 1] * tr2r[row])
        total = ig[row * COLS:(row + 1) * COLS, :] + tn_dot(left, m_ref[...])
        fgrad_ref[row] = total.astype(BF16)

    begun2 = [ring_relay(k, orders[k][1], part2, rec3, rec4, WIN, begun2[k]) for k in range(3)]
    for k in range(3):
        dsum[k] = ring_sum(k, orders[k][1], part2, rec4, begun2[k])

    def z_place(zz):
        place = g * (8 * (y % 2) + 54 * zz) + (1 - g) * ((12 * y) % 16 + 27 * zz)
        start = (place // 16) * 16 - 16 * g * (zz // 3)
        return place, pl.multiple_of(start, 16)

    z_copies = []
    for k in range(3):
        _, start = z_place((z + k + 1) % 4)
        z_copies.append(send(dsum.at[:, pl.ds(start, 80), :], zrec.at[k], (g, z_other[k])))
    place, start = z_place(z)
    total = dsum[:, pl.ds(start, 80), :].astype(F32)
    for k in range(3):
        z_copies[k].wait_recv()
        total = total + zrec[k].astype(F32)
    esum[:, 0:80, :] = total
    esum[:, 80:88, :] = jnp.zeros((3, 8, 128), F32)
    for target in range(2):
        fin[target] = esum[:, pl.ds(place - start + 27 * target * g, 32), :]

    def final_copy(source, comp, device, s_index, r_index):
        return pltpu.make_async_remote_copy(
            src_ref=fin.at[source], dst_ref=out.at[comp], send_sem=ssem.at[s_index],
            recv_sem=rsem.at[r_index], device_id=device, device_id_type=MESH,
        )

    base = len(used)
    base_lat = lat - core
    near_copy = final_copy(1 - core, g, (g, mate), base, base)
    far_zero = final_copy(0, g, (1 - g, base_lat), base + 1, base + 1)
    far_one = final_copy(1, g, (1 - g, base_lat + 1), base + 2, base + 1)

    @pl.when(core == g)
    def _():
        near_copy.start()
        out[g] = fin[core]
        near_copy.wait_send()

    @pl.when(core != g)
    def _():
        far_zero.start()
        far_one.start()
        far_zero.wait_send()
        far_one.wait_send()
        final_copy(0, g, (g, mate), base, base).wait_recv()

    final_copy(0, 1 - g, (1 - g, lat), base + 1, base + 1).wait_recv()
    grads_ref[...] = out[...]
    for copy in used:
        copy.wait_send()


def local(
    fields, cotangent, ocean_kernels, atmos_kernels, ocean_surface, ocean_coupling,
    atmos_flux, atmos_coupling, row_map, wet_mask,
):
    del row_map
    is_ocean = lax.axis_index("grp") == 0
    core = lax.axis_index("lat") % 2

    def paired(rows):
        none = jnp.zeros_like(rows)
        return jnp.concatenate(
            [jnp.concatenate([rows, none], axis=1), jnp.concatenate([none, rows], axis=1)], axis=0
        )

    def single(rows):
        return jnp.concatenate([rows, jnp.zeros_like(rows)], axis=0)

    def twice(rows):
        return jnp.concatenate([rows, rows], axis=0)

    m16 = twice(jnp.where(is_ocean, paired(ocean_surface.T), single(atmos_flux.T)))
    c16 = twice(jnp.where(is_ocean, paired(ocean_coupling), single(atmos_coupling)))
    wet = wet_mask.astype(F32).reshape(2, COLS, 2)
    covered = wet[:, :, 0] + wet[:, :, 1]
    inverse = jnp.where(is_ocean, 1.0 / jnp.maximum(covered, 1.0), 1.0)
    wet0 = jnp.where(is_ocean, wet[:, :, 0], 1.0)
    wet1 = jnp.where(is_ocean, wet[:, :, 1], 0.0)
    masks = jnp.stack([wet0, wet1], axis=1)[:, :, None, :]
    masks = jnp.broadcast_to(masks, (2, 2, 4, COLS)).reshape(2, 8, COLS)
    wm = jnp.stack([masks, jnp.broadcast_to(inverse[:, None, :], (2, 8, COLS))], axis=1)

    vmem = pl.BlockSpec(memory_space=pltpu.VMEM)
    hbm = pl.BlockSpec(memory_space=pl.ANY)
    rows4 = pltpu.VMEM((4, COLS, CH), BF16)
    rows2 = pltpu.VMEM((2, COLS, CH), BF16)
    cat4 = pltpu.VMEM((4, COLS, 3 * CH), BF16)
    wide = pltpu.VMEM((2 * COLS, CH), F32)
    small2, small4 = pltpu.VMEM((2, 8, COLS), F32), pltpu.VMEM((4, 8, COLS), F32)

    def buf(*shape):
        return pltpu.VMEM(shape, BF16)

    next_field, field_grad, grads = pl.pallas_call(
        body,
        out_shape=(
            jax.ShapeDtypeStruct((2, COLS, CH), BF16),
            jax.ShapeDtypeStruct((2, COLS, CH), BF16),
            jax.ShapeDtypeStruct((2, 3, 32, 128), F32),
        ),
        in_specs=[vmem, vmem, hbm, hbm, vmem, vmem, vmem],
        out_specs=(vmem, vmem, vmem),
        scratch_shapes=[
            buf(2, 3, 3 * CH, CH), buf(2, 3, 576, 192),
            rows4, rows4, rows4, rows4, rows4, cat4, cat4, cat4, cat4,
            small4, small2, small4, small2, small2, wide, wide, wide,
            rows2, rows2, rows2, rows2, buf(512, CH), buf(512, 256), buf(3456, 512), buf(1856, 512),
            buf(3, 4, 4 * WIN, 128), buf(3, 2, 2 * WIN, 128), buf(3, 2, 4 * WIN, 128),
            buf(3, 4, WIN, 128), buf(3, 2, WIN // 2, 128), buf(3, 2, WIN, 128),
            buf(3, WIN, 128), buf(3, 3, 80, 128),
            pltpu.VMEM((3, 88, 128), F32), pltpu.VMEM((2, 3, 32, 128), F32),
            pltpu.VMEM((2, 3, 32, 128), F32),
            pltpu.SemaphoreType.DMA((2,)), pltpu.SemaphoreType.DMA((NSEM,)),
            pltpu.SemaphoreType.DMA((NSEM,)),
        ],
        compiler_params=pltpu.CompilerParams(
            collective_id=0, has_side_effects=True, vmem_limit_bytes=56 * 1024 * 1024
        ),
        cost_estimate=pl.CostEstimate(
            flops=4_100_000_000, bytes_accessed=8_000_000, transcendentals=100_000
        ),
    )(
        fields[0], cotangent[0], atmos_kernels.reshape(2, 3, 3 * CH, CH),
        ocean_kernels.reshape(2, 3, 576, 192), m16, c16, wm,
    )
    flat = grads.transpose(0, 2, 1, 3).reshape(2, 32, CH)
    atmos_total = flat[1, :27].reshape(-1) * (1.0 / math.sqrt(256 * 128))
    ocean_pair = flat[0, :27, :192].reshape(2, 2592)
    ocean_total = jnp.where(core == 0, ocean_pair[0], ocean_pair[1]) * (1.0 / 256.0)
    return (next_field[None], field_grad[None], ocean_total, atmos_total)


def solution(mesh):
    in_specs = (
        P("grp", "lat", None, None),
        P("grp", "lat", None, None),
        P(),
        P(),
        P(),
        P(),
        P(),
        P(),
        P("lat"),
        P("lat", None),
    )
    out_specs = (
        P("grp", "lat", None, None),
        P("grp", "lat", None, None),
        P(("grp", "lat")),
        P(("grp", "lat")),
    )
    return jax.shard_map(local, mesh=mesh, in_specs=in_specs, out_specs=out_specs, check_vma=False)
```

profile of v0, /device:TPU:1, one launch (start us, length us, event | category | flops | bytes accessed | tf_op | source)
XLA Modules:
  0.0 77.6 jit_solution(6508739707003407112)
XLA Ops:
  0.6 0.7 convert_element_type.3
  1.3 0.1 reshape.63
  1.5 0.2 select_reduce_fusion.2
  1.8 0.6 pad_maximum_fusion.wm_ref
  2.4 0.8 %fusion.7 = (bf16[8,384]{1,0:T(8,128)(2,1)S(1)}, bf16[8,384]{1,0:T(8,128)(2,1)S(1)}) fusion(bf16[4,192]{1,0:T(4,128)(2,1)} %bitcast.23, bf16[4,384]{1,0:T(4,128)(2,1)} %bitcast.22, pred[]{:T(512)S(6)} %eq.8, bf16[4,384]{1,0:T(4,128)(2,1)} %param.17, bf16[4,192]{1,0:T(4,128)(2,1)} %param.15), kind=kLoop, calls=%fused_computation.18 | loop fusion | flops 49152 | bytes 21505 | tf_op jit(solution)/shard_map/jit(_where)/select_n | solution.py:444
  3.2 0.6 pad_maximum_fusion.1.m_ref
  3.8 0.6 pad_maximum_fusion.2.c_ref
  4.4 67.6 %shard_map.120 = (bf16[2,128,384]{2,1,0:T(8,128)(2,1)}, bf16[2,128,384]{2,1,0:T(8,128)(2,1)}, f32[2,3,32,128]{3,2,1,0:T(8,128)}) custom-call(bf16[2,128,384]{2,1,0:T(8,128)(2,1)} %bitcast.26, bf16[2,128,384]{2,1,0:T(8,128)(2,1)} %bitcast.27, bf16[2,3,1152,384]{3,2,1,0:T(8,128)(2,1)} %bitcast.24, bf16[2,3,576,192]{3,2,1,0:T(8,128)(2,1)} %bitcast.25, ...), custom_call_target="tpu_custom_call" | custom-call | flops 4100000000 | bytes 8000000 | tf_op jit(solution)/shard_map/pallas_call | solution.py:466
  72.0 0.9 %copy_bitcast_fusion = f32[2,32,384]{2,1,0:T(8,128)S(1)} fusion(f32[2,3,32,128]{3,2,1,0:T(8,128)} %get-tuple-element.9), kind=kLoop, calls=%fused_computation.3 | loop fusion | bytes 196608 | tf_op jit(solution)/shard_map/reshape | solution.py:498
  72.9 0.1 reshape_squeeze.4
  73.0 0.6 fusion.5
  73.7 0.6 mul.23
  74.3 1.6 %copy.29 = bf16[1,2,128,384]{3,2,1,0:T(8,128)(2,1)} copy(bf16[1,2,128,384]{3,2,1,0:T(8,128)(2,1)} %bitcast.18) | data formatting | bytes 393216
  75.9 1.6 %copy.30 = bf16[1,2,128,384]{3,2,1,0:T(8,128)(2,1)} copy(bf16[1,2,128,384]{3,2,1,0:T(8,128)(2,1)} %bitcast.17) | data formatting | bytes 393216
  (6 shorter events, 0.0 us)
where the time goes:
time: 78.3 us; the launch traced here: 77.6 us
  Pallas kernels  67.6 us (86%)
  local copies, waits for them, and re-layouts  5.01 us (6%)
  other arithmetic  4.23 us (5%)
    pallas_call x1, Pallas kernels, local(): pl.pallas_call(body, out_shape=(jax.ShapeDtypeStruct((2, COLS, CH), BF16)...  67.6 us
    unnamed x2, local copies, waits for them, and re-layouts  3.25 us

commit v1 on v0

v1 whole, which is shorter than its diff:
```python
import math

import jax
import jax.numpy as jnp
from jax import lax
from jax.experimental import pallas as pl
from jax.experimental.pallas import tpu as pltpu
from jax.sharding import PartitionSpec as P

MESH = pl.DeviceIdType.MESH
F32 = jnp.float32
BF16 = jnp.bfloat16
GELU_SCALE = 0.7978845608028654
GELU_CUBIC = 0.044715
CH = 384
COLS = 128
WIN = 224
NSEM = 64


def nt_dot(a, b):
    return lax.dot_general(a, b, (((1,), (1,)), ((), ())), preferred_element_type=F32)


def tn_dot(a, b):
    return lax.dot_general(a, b, (((0,), (0,)), ((), ())), preferred_element_type=F32)


def mm(a, b):
    return jnp.dot(a, b, preferred_element_type=F32)


def split_pair(values):
    high = values.astype(BF16).astype(F32)
    return jnp.concatenate([high, values - high], axis=0).astype(BF16)


def body(
    x_ref, g_ref, ak_ref, ok_ref, os_ref, oc_ref, af_ref, ac_ref, wet_ref,
    next_ref, fgrad_ref, grads_ref,
    w, okv, xp, gp, hp, fp, up, gcat, ucat, hcat, fcat, acat,
    m8, c8, m16, c16, wm, wmp, trs, trp, tr2s, tr2r, bh, ig,
    s_a, r_a, s_b, r_b, b6, b6s, at, at2,
    part, rec1, rec2, part2, rec3, rec4, dsum, zsend, zrec,
    wsem, ssem, rsem,
):
    g = lax.axis_index("grp")
    lat = lax.axis_index("lat")
    core = lat % 2
    z = (lat // 2) % 4
    y = (lat // 8) % 4
    x = lat // 32

    def spot(xx, yy, zz, cc):
        return xx * 32 + yy * 8 + zz * 2 + cc

    dn = (lat + 1) % 128
    up_lat = (lat + 127) % 128
    x_plus, x_minus = spot((x + 1) % 4, y, z, core), spot((x + 3) % 4, y, z, core)
    y_plus, y_minus = spot(x, (y + 1) % 4, z, core), spot(x, (y + 3) % 4, z, core)
    mate = lat + 1 - 2 * core
    has_top = jnp.where(lat > 0, 1.0, 0.0).astype(F32)
    has_low = jnp.where(lat < 127, 1.0, 0.0).astype(F32)
    edge = [has_top, None, None, has_low]

    atmos_copy = pltpu.make_async_copy(ak_ref, w, wsem.at[0])
    ocean_copy = pltpu.make_async_copy(ok_ref, okv, wsem.at[1])

    @pl.when(g == 1)
    def _():
        atmos_copy.start()

    @pl.when(g == 0)
    def _():
        ocean_copy.start()

    barrier = pltpu.get_barrier_semaphore()
    partners = [(g, dn), (g, up_lat), (1 - g, dn), (1 - g, up_lat)]
    partners += [(g, other) for other in (x_plus, x_minus, y_plus, y_minus)]
    for step in range(16):
        if step > 0:
            hop = (step // 2) % 4
            partners.append(
                ((g + step // 8) % 2, spot(x, y, (z + hop) % 4, (core + step) % 2))
            )
    for device in partners:
        pl.semaphore_signal(barrier, inc=1, device_id=device, device_id_type=MESH)

    half = CH // 2
    row_id = lax.broadcasted_iota(jnp.int32, (half, CH), 0)
    lane_id = lax.broadcasted_iota(jnp.int32, (half, CH), 1)
    lower = jnp.where(row_id == lane_id, 1.0, 0.0).astype(BF16)
    upper = jnp.where(row_id + half == lane_id, 1.0, 0.0).astype(BF16)
    is_atmos = g.astype(F32)
    is_ocean = 1.0 - is_atmos
    for dst, ocean, atmos in ((m8, os_ref, af_ref), (c8, oc_ref, ac_ref)):
        dst[0:4] = mm(ocean[...], lower) * is_ocean + atmos[...].astype(F32) * is_atmos
        dst[4:8] = mm(ocean[...], upper) * is_ocean
    for dst, src in ((m16, m8), (c16, c8)):
        dst[...] = jnp.concatenate([src[...], src[...]], axis=0).astype(BF16)
    pick_row = lax.broadcasted_iota(jnp.int32, (256, 256), 0)
    pick_lane = lax.broadcasted_iota(jnp.int32, (256, 256), 1)
    pick_lane = jnp.where(pick_lane < COLS, 2 * pick_lane, 2 * pick_lane - 255)
    pick = jnp.where(pick_row == pick_lane, 1.0, 0.0).astype(BF16)
    first_half = lax.broadcasted_iota(jnp.int32, (8, COLS), 0) < 4
    for row in range(2):
        wet = jnp.broadcast_to(wet_ref[row:row + 1, :].astype(F32), (8, 256)).astype(BF16)
        apart = mm(wet, pick)
        even, odd = apart[:, 0:COLS], apart[:, COLS:]
        inverse = 1.0 / jnp.maximum(even + odd, 1.0)
        wm[row, 0] = jnp.where(
            first_half, even * is_ocean + is_atmos, odd * is_ocean
        )
        wm[row, 1] = inverse * is_ocean + is_atmos

    for row in range(2):
        shown = nt_dot(m16[...], x_ref[row])[0:8] * wm[row, 0]
        trs[row] = (shown + pltpu.roll(shown, 4, 0)) * wm[row, 1]
    pl.semaphore_wait(barrier, len(partners))

    used = []

    def arrive(copy):
        copy.wait_recv()

    def send(src, dst, device):
        index = len(used)
        copy = pltpu.make_async_remote_copy(
            src_ref=src, dst_ref=dst, send_sem=ssem.at[index], recv_sem=rsem.at[index],
            device_id=device, device_id_type=MESH,
        )
        copy.start()
        used.append(copy)
        return copy

    t_mid = send(trs, trp.at[pl.ds(1, 2)], (1 - g, lat))
    t_low = send(trs.at[1], trp.at[0], (1 - g, dn))
    t_top = send(trs.at[0], trp.at[3], (1 - g, up_lat))
    m_low = send(wm.at[1, 0], wmp.at[0], (g, dn))
    m_top = send(wm.at[0, 0], wmp.at[3], (g, up_lat))
    x_low = send(x_ref.at[1], xp.at[0], (g, dn))
    x_top = send(x_ref.at[0], xp.at[3], (g, up_lat))
    g_low = send(g_ref.at[1], gp.at[0], (g, dn))
    g_top = send(g_ref.at[0], gp.at[3], (g, up_lat))

    column = lax.broadcasted_iota(jnp.int32, (COLS, CH), 0)

    def put_cat(dst, index, values):
        dst[index, :, CH:2 * CH] = values.astype(BF16)
        dst[index, :, 0:CH] = jnp.where(column > 0, pltpu.roll(values, 1, 0), 0.0).astype(BF16)
        dst[index, :, 2 * CH:3 * CH] = jnp.where(
            column < COLS - 1, pltpu.roll(values, COLS - 1, 0), 0.0
        ).astype(BF16)

    def conv(cat, layer):
        total = None
        for p in range(3):
            term = mm(cat[p:p + 2].reshape(2 * COLS, 3 * CH), w[layer, p])
            total = term if total is None else total + term
        return total

    def back_rows(cat, layer, p, row, count):
        total = None
        for q in range(3):
            rows = cat[row:row + count, :, q * CH:(q + 1) * CH].reshape(count * COLS, CH)
            term = nt_dot(rows, w[layer, 2 - p, (2 - q) * CH:(3 - q) * CH, :])
            total = term if total is None else total + term
        return total

    @pl.when(g == 0)
    def _():
        ocean_copy.wait()
        for layer in range(2):
            for p in range(3):
                low = mm(okv[layer, p], lower)
                high = mm(okv[layer, p], upper)
                none = jnp.zeros((half, CH), F32)
                both = jnp.concatenate([low, none], axis=0) + jnp.concatenate([none, high], axis=0)
                w[layer, p, 0:half, :] = none.astype(BF16)
                w[layer, p, half:5 * half, :] = both.astype(BF16)
                w[layer, p, 5 * half:6 * half, :] = none.astype(BF16)

    @pl.when(g == 1)
    def _():
        atmos_copy.wait()

    for row in range(2):
        put_cat(gcat, row + 1, g_ref[row].astype(F32))
    bh[...] = back_rows(gcat, 1, 1, 1, 2)
    bh[0:COLS] += back_rows(gcat, 1, 2, 2, 1)
    bh[COLS:] += back_rows(gcat, 1, 0, 1, 1)

    for copy in (m_low, m_top, t_mid, t_low, t_top, x_low, x_top):
        arrive(copy)
    for index in range(4):
        values = xp[index] if index in (0, 3) else x_ref[index - 1]
        mask = wmp[index] if index in (0, 3) else wm[index - 1, 0]
        term = tn_dot(split_pair(mask * trp[index]), c16[...])
        total = (values.astype(F32) + term).astype(BF16).astype(F32)
        if edge[index] is not None:
            total = total * edge[index]
        up[index] = total.astype(BF16)
        put_cat(ucat, index, total)
    zed = conv(ucat, 0)

    arrive(g_low)
    arrive(g_top)
    top_values = gp[0].astype(F32) * has_top
    low_values = gp[3].astype(F32) * has_low
    gp[0] = top_values.astype(BF16)
    gp[3] = low_values.astype(BF16)
    put_cat(gcat, 0, top_values)
    put_cat(gcat, 3, low_values)

    @pl.when(core == 0)
    def _():
        s_a[0] = gp[0]
        s_a[1] = g_ref[0]

    @pl.when(core == 1)
    def _():
        s_a[...] = up[2:4]

    pair_a = send(s_a, r_a, (g, mate))
    bh[0:COLS] += back_rows(gcat, 1, 0, 0, 1)
    bh[COLS:] += back_rows(gcat, 1, 2, 3, 1)

    tangent = jnp.tanh(GELU_SCALE * (zed + GELU_CUBIC * zed * zed * zed))
    hidden = (0.5 * zed * (1.0 + tangent)).astype(BF16).reshape(2, COLS, CH)
    slope = 0.5 * (1.0 + tangent) + 0.5 * zed * (1.0 - tangent * tangent) * GELU_SCALE * (
        1.0 + 3.0 * GELU_CUBIC * zed * zed
    )
    first_grad = (bh[...] * slope).astype(BF16).reshape(2, COLS, CH)
    hp[1:3] = hidden
    fp[1:3] = first_grad

    @pl.when(core == 0)
    def _():
        s_b[...] = hp[1:3]

    @pl.when(core == 1)
    def _():
        s_b[...] = fp[1:3]

    pair_b = send(s_b, r_b, (g, mate))
    h_low = send(hp.at[2], hp.at[0], (g, dn))
    h_top = send(hp.at[1], hp.at[3], (g, up_lat))
    f_low = send(fp.at[2], fp.at[0], (g, dn))
    f_top = send(fp.at[1], fp.at[3], (g, up_lat))

    def put_turned(source, places):
        turned = source.astype(F32).T.astype(BF16)

        @pl.when(g == 1)
        def _():
            for block, k in places:
                at[3 * CH * block:3 * CH * (block + 1), k * COLS:(k + 1) * COLS] = turned

        @pl.when(g == 0)
        def _():
            for block, k in places:
                at[576 * block:576 * (block + 1), k * COLS:(k + 1) * COLS] = turned[192:768]
                at2[576 * block:576 * (block + 1), k * COLS:(k + 1) * COLS] = turned[384:960]

    for row in (1, 2):
        put_cat(hcat, row, hp[row].astype(F32))

    arrive(pair_a)

    @pl.when(core == 0)
    def _():
        put_cat(acat, 0, r_a[0].astype(F32))
        put_cat(acat, 1, r_a[1].astype(F32))
        for index in range(6):
            places = [(p, index - p) for p in range(3) if 0 <= index - p <= 3]
            put_turned(ucat[index] if index < 4 else acat[index - 4], places)
        b6[0:256] = fp[1:3].reshape(256, CH)

    @pl.when(core == 1)
    def _():
        for row in (1, 2):
            put_turned(hcat[row], [(0, row + 1)])
        b6[0:256] = r_a[...].reshape(256, CH)
        b6[256:384] = gp[0]
        b6[384:640] = g_ref[...].reshape(256, CH)
        b6[640:768] = gp[3]

    arrive(pair_b)

    @pl.when(core == 0)
    def _():
        b6[256:512] = r_b[...].reshape(256, CH)

    @pl.when(core == 1)
    def _():
        for row in range(2):
            put_cat(acat, row, r_b[row].astype(F32))
            put_turned(acat[row], [(0, row)])

    @pl.when(g == 0)
    def _():
        swap_row = lax.broadcasted_iota(jnp.int32, (CH, 256), 0)
        swap_lane = lax.broadcasted_iota(jnp.int32, (CH, 256), 1)
        swap = jnp.where(swap_row == swap_lane + 192, 1.0, 0.0).astype(BF16)
        b6s[...] = mm(b6[...], swap).astype(BF16)


    ids_x, ids_y = (x, x_plus, x_minus), (y, y_plus, y_minus)
    mixed_a = tuple(a + core * (b - a) for a, b in zip(ids_x, ids_y))
    mixed_b = tuple(b + core * (a - b) for a, b in zip(ids_x, ids_y))
    orders = [(ids_x, ids_y), (ids_y, ids_x), (mixed_a, mixed_b)]

    atmos_pieces = [
        [(0, 0, 0, 224), (208, 1, 0, 80)],
        [(0, 1, 80, 144), (144, 2, 0, 144)],
        [(0, 2, 144, 80), (64, 3, 0, 224)],
    ]
    ocean_pieces = [
        [(0, 0, 0, 112), (96, 1, 0, 48)],
        [(0, 1, 48, 80), (64, 2, 0, 80)],
        [(0, 2, 80, 48), (32, 3, 0, 112)],
    ]

    def gradient_block(xq):
        def place(j, rows):
            m = 3 * xq + j
            start = rows * (m + core * (m % 4 - m))
            return (
                pl.ds(pl.multiple_of(start, 16), rows),
                pl.ds(pl.multiple_of(core * (2 - m // 4) * COLS, 16), 512),
            )

        def store(lane, made, pieces):
            for src, yq, dst, count in pieces:
                if lane == 0:
                    a, b = xq, yq
                elif lane == 1:
                    a, b = yq, xq
                else:
                    a, b = xq + core * (yq - xq), yq + core * (xq - yq)
                rows = pl.ds(pl.multiple_of(b * WIN + dst, 16), count)
                part[lane, a, rows, :] = made[src:src + count]

        @pl.when(g == 1)
        def _():
            for j in range(3):
                left, right = place(j, 288)
                made = mm(at[left, :], b6[right, :]).astype(BF16)
                for lane in range(3):
                    store(lane, made[:, 128 * lane:128 * (lane + 1)], atmos_pieces[j])

        @pl.when(g == 0)
        def _():
            for j in range(3):
                left, right = place(j, 144)
                made = mm(at[left, :], b6[right, 0:256]) + mm(at2[left, :], b6s[right, :])
                made = made.astype(BF16)
                for lane in range(2):
                    store(lane, made[:, 128 * lane:128 * (lane + 1)], ocean_pieces[j])

    def parts_of(rows):
        return pl.ds(0, rows // 2), pl.ds(rows // 2, rows // 2)

    def ring_one(lane, ids, source, near, rows):
        me, plus, minus = ids
        low, high = parts_of(rows)
        across = (me + 2) % 4
        one_p = send(source.at[lane, across, low], near.at[lane, 0], (g, plus))
        one_m = send(source.at[lane, across, high], near.at[lane, 1], (g, minus))
        return one_p, one_m

    def ring_two(lane, ids, source, far, rows, plus_side):
        me, plus, minus = ids
        low, high = parts_of(rows)
        if plus_side:
            return send(source.at[lane, (me + 1) % 4, high], far.at[lane, 0, high], (g, plus))
        return send(source.at[lane, (me + 3) % 4, low], far.at[lane, 1, low], (g, minus))

    def ring_relay(lane, ids, source, near, far, rows, early):
        me, plus, minus = ids
        low, high = parts_of(rows)
        ahead, behind = (me + 1) % 4, (me + 3) % 4
        arrive(early[0])
        source[lane, ahead, low, :] = (
            source[lane, ahead, low, :].astype(F32) + near[lane, 0].astype(F32)
        ).astype(BF16)
        three_p = send(source.at[lane, ahead, low], far.at[lane, 0, low], (g, plus))
        arrive(early[1])
        source[lane, behind, high, :] = (
            source[lane, behind, high, :].astype(F32) + near[lane, 1].astype(F32)
        ).astype(BF16)
        three_m = send(source.at[lane, behind, high], far.at[lane, 1, high], (g, minus))
        return three_p, three_m

    def ring_sum(lane, ids, source, far, late):
        for copy in late:
            arrive(copy)
        me = ids[0]
        return source[lane, me].astype(F32) + far[lane, 0].astype(F32) + far[lane, 1].astype(F32)

    early, middle, late = [None] * 3, [None] * 3, [None] * 3
    gradient_block((x + 2) % 4)
    early[0] = ring_one(0, orders[0][0], part, rec1, 4 * WIN)
    gradient_block((x + 1) % 4)
    gradient_block((x + 3) % 4)
    gradient_block(x)
    for k in (1, 2):
        early[k] = ring_one(k, orders[k][0], part, rec1, 4 * WIN)
    for k in range(3):
        middle[k] = tuple(
            ring_two(k, orders[k][0], part, rec2, 4 * WIN, side) for side in (True, False)
        )

    arrive(h_low)
    arrive(h_top)
    put_cat(hcat, 0, hp[0].astype(F32) * has_top)
    put_cat(hcat, 3, hp[3].astype(F32) * has_low)
    next_ref[...] = (up[1:3].astype(F32) + conv(hcat, 1).reshape(2, COLS, CH)).astype(BF16)
    for k in range(3):
        late[k] = ring_relay(k, orders[k][0], part, rec1, rec2, 4 * WIN, early[k])

    for row in (1, 2):
        put_cat(fcat, row, fp[row].astype(F32))
    arrive(f_low)
    arrive(f_top)
    put_cat(fcat, 0, fp[0].astype(F32) * has_top)
    put_cat(fcat, 3, fp[3].astype(F32) * has_low)
    total = g_ref[...].reshape(2 * COLS, CH).astype(F32)
    for p in range(3):
        total = total + back_rows(fcat, 0, p, p, 2)
    ig[...] = total

    for row in range(2):
        grad = ig[row * COLS:(row + 1) * COLS, :]
        high = grad.astype(BF16)
        low = (grad - high.astype(F32)).astype(BF16)
        shown = (nt_dot(c16[...], high) + nt_dot(c16[...], low))[0:8] * wm[row, 0]
        tr2s[row] = shown + pltpu.roll(shown, 4, 0)
    back = send(tr2s, tr2r, (1 - g, lat))

    early2, middle2 = [], []
    for k in range(3):
        made = ring_sum(k, orders[k][0], part, rec2, middle[k] + late[k])
        part2[k] = made.astype(BF16).reshape(4, WIN, 128)
        early2.append(ring_one(k, orders[k][1], part2, rec3, WIN))
        middle2.append(tuple(
            ring_two(k, orders[k][1], part2, rec4, WIN, side) for side in (True, False)
        ))
    late2 = [
        ring_relay(k, orders[k][1], part2, rec3, rec4, WIN, early2[k]) for k in range(3)
    ]
    for k in range(3):
        dsum[k, 0:WIN] = ring_sum(k, orders[k][1], part2, rec4, middle2[k] + late2[k])

    base = len(used)

    def z_copy(slot, comp, k, device, index):
        return pltpu.make_async_remote_copy(
            src_ref=zsend.at[slot], dst_ref=zrec.at[comp, k], send_sem=ssem.at[base + index],
            recv_sem=rsem.at[base + comp * 4 + k], device_id=device, device_id_type=MESH,
        )

    dsum[:, WIN:WIN + 16] = jnp.zeros((3, 16, 128), F32)
    for hop in range(4):
        zz = (z + hop) % 4
        place = g * (8 * (y % 2) + 54 * zz) + (1 - g) * ((12 * y) % 16 + 27 * zz)
        for cc in range(2):
            slot = 2 * hop + cc
            zsend[slot] = dsum[:, pl.ds(place + 27 * cc * g, 32), :].astype(BF16)
            copy = z_copy(slot, g, (4 - hop) % 4, (core, spot(x, y, zz, cc)), slot)
            if hop > 0:
                copy.start()
            else:
                @pl.when((core != g) | (core != cc))
                def _():
                    copy.start()

    for row in range(2):
        if row == 0:
            arrive(back)
        left = split_pair(wm[row, 0] * wm[row, 1] * tr2r[row])
        total = ig[row * COLS:(row + 1) * COLS, :] + tn_dot(left, m16[...])
        fgrad_ref[row] = total.astype(BF16)

    @pl.when(core == g)
    def _():
        zrec[g, 0] = zsend[core]

    for comp in range(2):
        for k in range(4):
            copy = z_copy(0, comp, k, (g, mate), 0)
            if k > 0:
                copy.wait_recv()
            else:
                @pl.when((core != g) | (g != comp))
                def _():
                    copy.wait_recv()

        total = zrec[comp, 0].astype(F32)
        for k in range(1, 4):
            total = total + zrec[comp, k].astype(F32)
        grads_ref[comp] = total
    for hop in range(4):
        for cc in range(2):
            slot = 2 * hop + cc
            copy = z_copy(slot, g, 0, (g, mate), slot)
            if hop > 0:
                copy.wait_send()
            else:
                @pl.when((core != g) | (core != cc))
                def _():
                    copy.wait_send()
    for copy in used:
        copy.wait_send()


def finish_body(next_in, fgrad_in, grads_in, next_out, fgrad_out, ocean_out, atmos_out, flat):
    next_out[0] = next_in[...]
    fgrad_out[0] = fgrad_in[...]
    atmos_factor = 1.0 / math.sqrt(256 * 128)
    for lane in range(3):
        atmos_out[pl.ds(lane, 27, stride=3), :] = grads_in[1, lane, 0:27, :] * atmos_factor
    left = lax.broadcasted_iota(jnp.int32, (14, 128), 1) < 64

    def rows(lane, start):
        return grads_in[0, lane, pl.ds(start, 14, stride=2), :] * (1.0 / 256.0)

    even_0, even_1, odd_0, odd_1 = rows(0, 0), rows(1, 0), rows(0, 1), rows(1, 1)
    odd_0, odd_1 = pltpu.roll(odd_0, 64, 1), pltpu.roll(odd_1, 64, 1)
    flat[pl.ds(0, 14, stride=3), :] = even_0
    flat[pl.ds(1, 14, stride=3), :] = jnp.where(left, even_1, odd_0)
    flat[pl.ds(2, 14, stride=3), :] = jnp.where(left, odd_0, odd_1)
    core = lax.axis_index("lat") % 2

    @pl.when(core == 0)
    def _():
        ocean_out[...] = flat[0:21]

    @pl.when(core == 1)
    def _():
        here = pltpu.roll(flat[20:41], 96, 1)
        after = pltpu.roll(flat[21:42], 96, 1)
        lanes = lax.broadcasted_iota(jnp.int32, (21, 128), 1)
        ocean_out[...] = jnp.where(lanes < 96, here, after)


def local(
    fields, cotangent, ocean_kernels, atmos_kernels, ocean_surface, ocean_coupling,
    atmos_flux, atmos_coupling, row_map, wet_mask,
):
    del row_map
    vmem = pl.BlockSpec(memory_space=pltpu.VMEM)
    hbm = pl.BlockSpec(memory_space=pl.ANY)
    rows4 = pltpu.VMEM((4, COLS, CH), BF16)
    rows2 = pltpu.VMEM((2, COLS, CH), BF16)
    cat4 = pltpu.VMEM((4, COLS, 3 * CH), BF16)
    wide = pltpu.VMEM((2 * COLS, CH), F32)
    small2, small4 = pltpu.VMEM((2, 8, COLS), F32), pltpu.VMEM((4, 8, COLS), F32)

    def buf(*shape):
        return pltpu.VMEM(shape, BF16)

    limits = dict(vmem_limit_bytes=56 * 1024 * 1024)
    next_field, field_grad, grads = pl.pallas_call(
        body,
        out_shape=(
            jax.ShapeDtypeStruct((2, COLS, CH), BF16),
            jax.ShapeDtypeStruct((2, COLS, CH), BF16),
            jax.ShapeDtypeStruct((2, 3, 32, 128), F32),
        ),
        in_specs=[vmem, vmem, hbm, hbm, vmem, vmem, vmem, vmem, vmem],
        out_specs=(vmem, vmem, vmem),
        scratch_shapes=[
            buf(2, 3, 3 * CH, CH), buf(2, 3, 576, 192),
            rows4, rows4, rows4, rows4, rows4, cat4, cat4, cat4, cat4,
            buf(2, COLS, 3 * CH),
            pltpu.VMEM((8, CH), F32), pltpu.VMEM((8, CH), F32), buf(16, CH), buf(16, CH),
            pltpu.VMEM((2, 2, 8, COLS), F32), small4, small2, small4, small2, small2, wide, wide,
            rows2, rows2, rows2, rows2, buf(768, CH), buf(768, 256), buf(3456, 512), buf(1728, 512),
            buf(3, 4, 4 * WIN, 128), buf(3, 2, 2 * WIN, 128), buf(3, 2, 4 * WIN, 128),
            buf(3, 4, WIN, 128), buf(3, 2, WIN // 2, 128), buf(3, 2, WIN, 128),
            pltpu.VMEM((3, 240, 128), F32), buf(8, 3, 32, 128), buf(2, 4, 3, 32, 128),
            pltpu.SemaphoreType.DMA((2,)), pltpu.SemaphoreType.DMA((NSEM,)),
            pltpu.SemaphoreType.DMA((NSEM,)),
        ],
        compiler_params=pltpu.CompilerParams(
            collective_id=0, has_side_effects=True, **limits
        ),
        cost_estimate=pl.CostEstimate(
            flops=4_100_000_000, bytes_accessed=8_000_000, transcendentals=100_000
        ),
    )(
        fields[0], cotangent[0], atmos_kernels.reshape(2, 3, 3 * CH, CH),
        ocean_kernels.reshape(2, 3, 576, 192), ocean_surface.T, ocean_coupling, atmos_flux.T,
        atmos_coupling, wet_mask,
    )
    next_field, field_grad, ocean_rows, atmos_rows = pl.pallas_call(
        finish_body,
        out_shape=(
            jax.ShapeDtypeStruct((1, 2, COLS, CH), BF16),
            jax.ShapeDtypeStruct((1, 2, COLS, CH), BF16),
            jax.ShapeDtypeStruct((21, 128), F32),
            jax.ShapeDtypeStruct((81, 128), F32),
        ),
        in_specs=[vmem, vmem, vmem],
        out_specs=(vmem, vmem, vmem, vmem),
        scratch_shapes=[pltpu.VMEM((48, 128), F32)],
    )(next_field, field_grad, grads)
    return (next_field, field_grad, ocean_rows.reshape(-1)[:2592], atmos_rows.reshape(-1))


def solution(mesh):
    in_specs = (
        P("grp", "lat", None, None),
        P("grp", "lat", None, None),
        P(),
        P(),
        P(),
        P(),
        P(),
        P(),
        P("lat"),
        P("lat", None),
    )
    out_specs = (
        P("grp", "lat", None, None),
        P("grp", "lat", None, None),
        P(("grp", "lat")),
        P(("grp", "lat")),
    )
    return jax.shard_map(local, mesh=mesh, in_specs=in_specs, out_specs=out_specs, check_vma=False)
```

time: 78.3 us -> 55.5 us (0.71)
  Pallas kernels: 67.6 us -> 54.7 us
  local copies, waits for them, and re-layouts: 5.01 us -> 0 us
  other arithmetic: 4.23 us -> 0 us
    pallas_call x1, Pallas kernels: 67.6 us -> 52.7 us  [local(): pl.pallas_call(body, out_shape=(jax.ShapeDtypeStruct((2, COLS, CH), BF16)...]
    unnamed x2 -> x0, local copies, waits for them, and re-layouts: 3.25 us -> none
    pallas_call x0 -> x1, Pallas kernels: none -> 2.03 us  [local(): pl.pallas_call(finish_body, out_shape=(jax.ShapeDtypeStruct((1, 2, COLS,...]
    concatenate x2 -> x0, other arithmetic: 1.2 us -> none  [twice(): return jnp.concatenate([rows, rows], axis=0)]
    select_n x2 -> x0, other arithmetic: 1.08 us -> none  [the longest x1 0.85 us: local(): jnp.where(is_ocean, paired(ocean_surface.T), single(atmos_flux.T))]
    reshape x2 -> x0, local copies, waits for them, and re-layouts: 1.04 us -> none  [the longest x1 0.9 us: local(): flat = grads.transpose(0, 2, 1, 3).reshape(2, 32, CH)]
where the time goes in v1:
time: 55.5 us; the launch traced here: 55.4 us
  Pallas kernels  54.7 us (99%)
  between operations  0.64 us (1%)
    pallas_call x1, Pallas kernels, local(): pl.pallas_call(body, out_shape=(jax.ShapeDtypeStruct((2, COLS, CH), BF16)...  52.7 us
    pallas_call x1, Pallas kernels, local(): pl.pallas_call(finish_body, out_shape=(jax.ShapeDtypeStruct((1, 2, COLS,...  2.03 us

profile of v1, /device:TPU:1, one launch (start us, length us, event | category | flops | bytes accessed | tf_op | source)
XLA Modules:
  0.0 55.4 jit_solution(3394001515458041888)
XLA Ops:
  0.6 52.7 %shard_map.120 = (bf16[2,128,384]{2,1,0:T(8,128)(2,1)}, bf16[2,128,384]{2,1,0:T(8,128)(2,1)}, f32[2,3,32,128]{3,2,1,0:T(8,128)}) custom-call(bf16[2,128,384]{2,1,0:T(8,128)(2,1)} %bitcast.11, bf16[2,128,384]{2,1,0:T(8,128)(2,1)} %bitcast.12, bf16[2,3,1152,384]{3,2,1,0:T(8,128)(2,1)} %bitcast.9, bf16[2,3,576,192]{3,2,1,0:T(8,128)(2,1)} %bitcast.10, ...), custom_call_target="tpu_custom_call" | custom-call | flops 4100000000 | bytes 8000000 | tf_op jit(solution)/shard_map/pallas_call | solution.py:564
  53.3 2.0 %shard_map.121 = (bf16[1,2,128,384]{3,2,1,0:T(8,128)(2,1)}, bf16[1,2,128,384]{3,2,1,0:T(8,128)(2,1)}, f32[21,128]{1,0:T(8,128)}, f32[81,128]{1,0:T(8,128)}) custom-call(bf16[2,128,384]{2,1,0:T(8,128)(2,1)} %get-tuple-element.11.next_in, bf16[2,128,384]{2,1,0:T(8,128)(2,1)} %get-tuple-element.12.fgrad_in, f32[2,3,32,128]{3,2,1,0:T(8,128)} %get-tuple-element.13.grads_in), custom_call_target="tpu_custom_call" | custom-call | tf_op jit(solution)/shard_map/pallas_call | solution.py:597

commit v2 on v1

--- a/solution.py
+++ b/solution.py
@@ -15,7 +15,7 @@
 CH = 384
 COLS = 128
 WIN = 224
-NSEM = 64
+NSEM = 80
 
 
 def nt_dot(a, b):
@@ -190,9 +190,7 @@
     bh[0:COLS] += back_rows(gcat, 1, 2, 2, 1)
     bh[COLS:] += back_rows(gcat, 1, 0, 1, 1)
 
-    for copy in (m_low, m_top, t_mid, t_low, t_top, x_low, x_top):
-        arrive(copy)
-    for index in range(4):
+    def layer_input(index):
         values = xp[index] if index in (0, 3) else x_ref[index - 1]
         mask = wmp[index] if index in (0, 3) else wm[index - 1, 0]
         term = tn_dot(split_pair(mask * trp[index]), c16[...])
@@ -201,7 +199,19 @@
             total = total * edge[index]
         up[index] = total.astype(BF16)
         put_cat(ucat, index, total)
-    zed = conv(ucat, 0)
+
+    arrive(t_mid)
+    layer_input(1)
+    layer_input(2)
+    ig[...] = mm(ucat[1:3].reshape(2 * COLS, 3 * CH), w[0, 1])
+    ig[0:COLS] += mm(ucat[2], w[0, 2])
+    ig[COLS:] += mm(ucat[1], w[0, 0])
+    for copy in (m_low, m_top, t_low, t_top, x_low, x_top):
+        arrive(copy)
+    layer_input(0)
+    layer_input(3)
+    ig[0:COLS] += mm(ucat[0], w[0, 0])
+    ig[COLS:] += mm(ucat[3], w[0, 2])
 
     arrive(g_low)
     arrive(g_top)
@@ -225,6 +235,7 @@
     bh[0:COLS] += back_rows(gcat, 1, 0, 0, 1)
     bh[COLS:] += back_rows(gcat, 1, 2, 3, 1)
 
+    zed = ig[...]
     tangent = jnp.tanh(GELU_SCALE * (zed + GELU_CUBIC * zed * zed * zed))
     hidden = (0.5 * zed * (1.0 + tangent)).astype(BF16).reshape(2, COLS, CH)
     slope = 0.5 * (1.0 + tangent) + 0.5 * zed * (1.0 - tangent * tangent) * GELU_SCALE * (
@@ -399,25 +410,102 @@
         return source[lane, me].astype(F32) + far[lane, 0].astype(F32) + far[lane, 1].astype(F32)
 
     early, middle, late = [None] * 3, [None] * 3, [None] * 3
+    early2, middle2, late2 = [None] * 3, [None] * 3, [None] * 3
+
+    def first_two(k):
+        middle[k] = tuple(
+            ring_two(k, orders[k][0], part, rec2, 4 * WIN, side) for side in (True, False)
+        )
+
+    def first_relay(k):
+        late[k] = ring_relay(k, orders[k][0], part, rec1, rec2, 4 * WIN, early[k])
+
+    def second_start(k):
+        made = ring_sum(k, orders[k][0], part, rec2, middle[k] + late[k])
+        part2[k] = made.astype(BF16).reshape(4, WIN, 128)
+        early2[k] = ring_one(k, orders[k][1], part2, rec3, WIN)
+        middle2[k] = tuple(
+            ring_two(k, orders[k][1], part2, rec4, WIN, side) for side in (True, False)
+        )
+
+    def second_relay(k):
+        late2[k] = ring_relay(k, orders[k][1], part2, rec3, rec4, WIN, early2[k])
+
+    base = 56
+
+    def z_copy(lane, slot, comp, k, device):
+        return pltpu.make_async_remote_copy(
+            src_ref=zsend.at[lane, slot], dst_ref=zrec.at[comp, k, lane],
+            send_sem=ssem.at[base + lane * 8 + slot],
+            recv_sem=rsem.at[base + lane * 8 + comp * 4 + k],
+            device_id=device, device_id_type=MESH,
+        )
+
+    def third_start(k):
+        dsum[0:WIN] = ring_sum(k, orders[k][1], part2, rec4, middle2[k] + late2[k])
+        dsum[WIN:WIN + 16] = jnp.zeros((16, 128), F32)
+        for hop in (2, 1, 3, 0):
+            zz = (z + hop) % 4
+            place = g * (8 * (y % 2) + 54 * zz) + (1 - g) * ((12 * y) % 16 + 27 * zz)
+            for cc in range(2):
+                slot = 2 * hop + cc
+                zsend[k, slot] = dsum[pl.ds(place + 27 * cc * g, 32), :].astype(BF16)
+                copy = z_copy(k, slot, g, (4 - hop) % 4, (core, spot(x, y, zz, cc)))
+                if hop > 0:
+                    copy.start()
+                else:
+                    @pl.when((core != g) | (core != cc))
+                    def _():
+                        copy.start()
+
+    def third_end(k):
+        @pl.when(core == g)
+        def _():
+            zrec[g, 0, k] = zsend[k, core]
+
+        for comp in range(2):
+            for source in range(4):
+                copy = z_copy(k, 0, comp, source, (g, mate))
+                if source > 0:
+                    copy.wait_recv()
+                else:
+                    @pl.when((core != g) | (g != comp))
+                    def _():
+                        copy.wait_recv()
+
+            total = zrec[comp, 0, k].astype(F32)
+            for source in range(1, 4):
+                total = total + zrec[comp, source, k].astype(F32)
+            grads_ref[comp, k] = total
+        for hop in range(4):
+            for cc in range(2):
+                slot = 2 * hop + cc
+                copy = z_copy(k, slot, g, 0, (g, mate))
+                if hop > 0:
+                    copy.wait_send()
+                else:
+                    @pl.when((core != g) | (core != cc))
+                    def _():
+                        copy.wait_send()
+
     gradient_block((x + 2) % 4)
     early[0] = ring_one(0, orders[0][0], part, rec1, 4 * WIN)
     gradient_block((x + 1) % 4)
     gradient_block((x + 3) % 4)
     gradient_block(x)
-    for k in (1, 2):
-        early[k] = ring_one(k, orders[k][0], part, rec1, 4 * WIN)
-    for k in range(3):
-        middle[k] = tuple(
-            ring_two(k, orders[k][0], part, rec2, 4 * WIN, side) for side in (True, False)
-        )
+    early[1] = ring_one(1, orders[1][0], part, rec1, 4 * WIN)
+    first_two(0)
+    first_two(1)
+    early[2] = ring_one(2, orders[2][0], part, rec1, 4 * WIN)
 
     arrive(h_low)
     arrive(h_top)
     put_cat(hcat, 0, hp[0].astype(F32) * has_top)
     put_cat(hcat, 3, hp[3].astype(F32) * has_low)
     next_ref[...] = (up[1:3].astype(F32) + conv(hcat, 1).reshape(2, COLS, CH)).astype(BF16)
-    for k in range(3):
-        late[k] = ring_relay(k, orders[k][0], part, rec1, rec2, 4 * WIN, early[k])
+    first_relay(0)
+    first_relay(1)
+    first_two(2)
 
     for row in (1, 2):
         put_cat(fcat, row, fp[row].astype(F32))
@@ -437,86 +525,35 @@
         shown = (nt_dot(c16[...], high) + nt_dot(c16[...], low))[0:8] * wm[row, 0]
         tr2s[row] = shown + pltpu.roll(shown, 4, 0)
     back = send(tr2s, tr2r, (1 - g, lat))
-
-    early2, middle2 = [], []
-    for k in range(3):
-        made = ring_sum(k, orders[k][0], part, rec2, middle[k] + late[k])
-        part2[k] = made.astype(BF16).reshape(4, WIN, 128)
-        early2.append(ring_one(k, orders[k][1], part2, rec3, WIN))
-        middle2.append(tuple(
-            ring_two(k, orders[k][1], part2, rec4, WIN, side) for side in (True, False)
-        ))
-    late2 = [
-        ring_relay(k, orders[k][1], part2, rec3, rec4, WIN, early2[k]) for k in range(3)
-    ]
-    for k in range(3):
-        dsum[k, 0:WIN] = ring_sum(k, orders[k][1], part2, rec4, middle2[k] + late2[k])
-
-    base = len(used)
-
-    def z_copy(slot, comp, k, device, index):
-        return pltpu.make_async_remote_copy(
-            src_ref=zsend.at[slot], dst_ref=zrec.at[comp, k], send_sem=ssem.at[base + index],
-            recv_sem=rsem.at[base + comp * 4 + k], device_id=device, device_id_type=MESH,
-        )
-
-    dsum[:, WIN:WIN + 16] = jnp.zeros((3, 16, 128), F32)
-    for hop in range(4):
-        zz = (z + hop) % 4
-        place = g * (8 * (y % 2) + 54 * zz) + (1 - g) * ((12 * y) % 16 + 27 * zz)
-        for cc in range(2):
-            slot = 2 * hop + cc
-            zsend[slot] = dsum[:, pl.ds(place + 27 * cc * g, 32), :].astype(BF16)
-            copy = z_copy(slot, g, (4 - hop) % 4, (core, spot(x, y, zz, cc)), slot)
-            if hop > 0:
-                copy.start()
-            else:
-                @pl.when((core != g) | (core != cc))
-                def _():
-                    copy.start()
-
+    first_relay(2)
+    second_start(0)
+    second_start(1)
+    second_relay(0)
+    second_relay(1)
+    second_start(2)
+    third_start(0)
+    third_start(1)
+    second_relay(2)
+    arrive(back)
     for row in range(2):
-        if row == 0:
-            arrive(back)
         left = split_pair(wm[row, 0] * wm[row, 1] * tr2r[row])
         total = ig[row * COLS:(row + 1) * COLS, :] + tn_dot(left, m16[...])
         fgrad_ref[row] = total.astype(BF16)
-
-    @pl.when(core == g)
-    def _():
-        zrec[g, 0] = zsend[core]
-
-    for comp in range(2):
-        for k in range(4):
-            copy = z_copy(0, comp, k, (g, mate), 0)
-            if k > 0:
-                copy.wait_recv()
-            else:
-                @pl.when((core != g) | (g != comp))
-                def _():
-                    copy.wait_recv()
-
-        total = zrec[comp, 0].astype(F32)
-        for k in range(1, 4):
-            total = total + zrec[comp, k].astype(F32)
-        grads_ref[comp] = total
-    for hop in range(4):
-        for cc in range(2):
-            slot = 2 * hop + cc
-            copy = z_copy(slot, g, 0, (g, mate), slot)
-            if hop > 0:
-                copy.wait_send()
-            else:
-                @pl.when((core != g) | (core != cc))
-                def _():
-                    copy.wait_send()
+    third_start(2)
+    assert len(used) <= base
+    for k in range(3):
+        third_end(k)
     for copy in used:
         copy.wait_send()
 
 
-def finish_body(next_in, fgrad_in, grads_in, next_out, fgrad_out, ocean_out, atmos_out, flat):
-    next_out[0] = next_in[...]
-    fgrad_out[0] = fgrad_in[...]
+def finish_body(next_in, fgrad_in, grads_in, next_out, fgrad_out, ocean_out, atmos_out, flat, sems):
+    copies = [
+        pltpu.make_async_copy(next_in, next_out.at[0], sems.at[0]),
+        pltpu.make_async_copy(fgrad_in, fgrad_out.at[0], sems.at[1]),
+    ]
+    for copy in copies:
+        copy.start()
     atmos_factor = 1.0 / math.sqrt(256 * 128)
     for lane in range(3):
         atmos_out[pl.ds(lane, 27, stride=3), :] = grads_in[1, lane, 0:27, :] * atmos_factor
@@ -542,6 +579,9 @@
         after = pltpu.roll(flat[21:42], 96, 1)
         lanes = lax.broadcasted_iota(jnp.int32, (21, 128), 1)
         ocean_out[...] = jnp.where(lanes < 96, here, after)
+
+    for copy in copies:
+        copy.wait()
 
 
 def local(
@@ -579,7 +619,7 @@
             rows2, rows2, rows2, rows2, buf(768, CH), buf(768, 256), buf(3456, 512), buf(1728, 512),
             buf(3, 4, 4 * WIN, 128), buf(3, 2, 2 * WIN, 128), buf(3, 2, 4 * WIN, 128),
             buf(3, 4, WIN, 128), buf(3, 2, WIN // 2, 128), buf(3, 2, WIN, 128),
-            pltpu.VMEM((3, 240, 128), F32), buf(8, 3, 32, 128), buf(2, 4, 3, 32, 128),
+            pltpu.VMEM((240, 128), F32), buf(3, 8, 32, 128), buf(2, 4, 3, 32, 128),
             pltpu.SemaphoreType.DMA((2,)), pltpu.SemaphoreType.DMA((NSEM,)),
             pltpu.SemaphoreType.DMA((NSEM,)),
         ],
@@ -602,9 +642,9 @@
             jax.ShapeDtypeStruct((21, 128), F32),
             jax.ShapeDtypeStruct((81, 128), F32),
         ),
-        in_specs=[vmem, vmem, vmem],
-        out_specs=(vmem, vmem, vmem, vmem),
-        scratch_shapes=[pltpu.VMEM((48, 128), F32)],
+        in_specs=[hbm, hbm, vmem],
+        out_specs=(hbm, hbm, vmem, vmem),
+        scratch_shapes=[pltpu.VMEM((48, 128), F32), pltpu.SemaphoreType.DMA((2,))],
     )(next_field, field_grad, grads)
     return (next_field, field_grad, ocean_rows.reshape(-1)[:2592], atmos_rows.reshape(-1))
 

time: 55.5 us -> 69.5 us (1.25)
  Pallas kernels: 54.7 us -> 68.6 us
    pallas_call x1, Pallas kernels: 2.03 us -> 14.5 us  [local(): pl.pallas_call(finish_body, out_shape=(jax.ShapeDtypeStruct((1, 2, COLS,...]
    pallas_call x1, Pallas kernels: 52.7 us -> 54 us  [local(): pl.pallas_call(body, out_shape=(jax.ShapeDtypeStruct((2, COLS, CH), BF16)...]
where the time goes in v2:
time: 69.5 us; the launch traced here: 69.4 us
  Pallas kernels  68.6 us (99%)
  between operations  0.8 us (1%)
    pallas_call x1, Pallas kernels, local(): pl.pallas_call(body, out_shape=(jax.ShapeDtypeStruct((2, COLS, CH), BF16)...  54 us
    pallas_call x1, Pallas kernels, local(): pl.pallas_call(finish_body, out_shape=(jax.ShapeDtypeStruct((1, 2, COLS,...  14.5 us

profile of v2, /device:TPU:1, one launch (start us, length us, event | category | flops | bytes accessed | tf_op | source)
XLA Modules:
  0.0 69.4 jit_solution(1069108704119609176)
XLA Ops:
  0.6 54.0 %shard_map.120 = (bf16[2,128,384]{2,1,0:T(8,128)(2,1)}, bf16[2,128,384]{2,1,0:T(8,128)(2,1)}, f32[2,3,32,128]{3,2,1,0:T(8,128)}) custom-call(bf16[2,128,384]{2,1,0:T(8,128)(2,1)} %bitcast.11, bf16[2,128,384]{2,1,0:T(8,128)(2,1)} %bitcast.12, bf16[2,3,1152,384]{3,2,1,0:T(8,128)(2,1)} %bitcast.9, bf16[2,3,576,192]{3,2,1,0:T(8,128)(2,1)} %bitcast.10, ...), custom_call_target="tpu_custom_call" | custom-call | flops 4100000000 | bytes 8000000 | tf_op jit(solution)/shard_map/pallas_call | solution.py:604
  54.7 14.5 %shard_map.121 = (bf16[1,2,128,384]{3,2,1,0:T(8,128)(2,1)}, bf16[1,2,128,384]{3,2,1,0:T(8,128)(2,1)}, f32[21,128]{1,0:T(8,128)}, f32[81,128]{1,0:T(8,128)}) custom-call(bf16[2,128,384]{2,1,0:T(8,128)(2,1)} %get-tuple-element.11.next_in, bf16[2,128,384]{2,1,0:T(8,128)(2,1)} %get-tuple-element.12.fgrad_in, f32[2,3,32,128]{3,2,1,0:T(8,128)} %get-tuple-element.13.grads_in), custom_call_target="tpu_custom_call" | custom-call | tf_op jit(solution)/shard_map/pallas_call | solution.py:637

commit v3 on v2

--- a/solution.py
+++ b/solution.py
@@ -36,11 +36,11 @@
 
 
 def body(
-    x_ref, g_ref, ak_ref, ok_ref, os_ref, oc_ref, af_ref, ac_ref, wet_ref,
+    x_hbm, g_hbm, ak_ref, ok_ref, os_ref, oc_ref, af_ref, ac_ref, wet_ref,
     next_ref, fgrad_ref, grads_ref,
-    w, okv, xp, gp, hp, fp, up, gcat, ucat, hcat, fcat, acat,
-    m8, c8, m16, c16, wm, wmp, trs, trp, tr2s, tr2r, bh, ig,
-    s_a, r_a, s_b, r_b, b6, b6s, at, at2,
+    x_ref, g_ref, w, okv, xp, gp, hp, fp, up, gcat, ucat, hcat,
+    wt, ft, m8, c8, m16, c16, wm, wmp, trs, trp, tr2s, tr2r, bh, ig,
+    s_a, r_a, s_b, r_b, b6, b6s, at6,
     part, rec1, rec2, part2, rec3, rec4, dsum, zsend, zrec,
     wsem, ssem, rsem,
 ):
@@ -63,16 +63,10 @@
     has_low = jnp.where(lat < 127, 1.0, 0.0).astype(F32)
     edge = [has_top, None, None, has_low]
 
-    atmos_copy = pltpu.make_async_copy(ak_ref, w, wsem.at[0])
-    ocean_copy = pltpu.make_async_copy(ok_ref, okv, wsem.at[1])
-
-    @pl.when(g == 1)
-    def _():
-        atmos_copy.start()
-
-    @pl.when(g == 0)
-    def _():
-        ocean_copy.start()
+    x_copy = pltpu.make_async_copy(x_hbm, x_ref, wsem.at[2])
+    g_copy = pltpu.make_async_copy(g_hbm, g_ref, wsem.at[3])
+    x_copy.start()
+    g_copy.start()
 
     barrier = pltpu.get_barrier_semaphore()
     partners = [(g, dn), (g, up_lat), (1 - g, dn), (1 - g, up_lat)]
@@ -85,6 +79,17 @@
             )
     for device in partners:
         pl.semaphore_signal(barrier, inc=1, device_id=device, device_id_type=MESH)
+
+    atmos_copy = pltpu.make_async_copy(ak_ref, w, wsem.at[0])
+    ocean_copy = pltpu.make_async_copy(ok_ref, okv, wsem.at[1])
+
+    @pl.when(g == 1)
+    def _():
+        atmos_copy.start()
+
+    @pl.when(g == 0)
+    def _():
+        ocean_copy.start()
 
     half = CH // 2
     row_id = lax.broadcasted_iota(jnp.int32, (half, CH), 0)
@@ -113,9 +118,11 @@
         )
         wm[row, 1] = inverse * is_ocean + is_atmos
 
+    x_copy.wait()
     for row in range(2):
         shown = nt_dot(m16[...], x_ref[row])[0:8] * wm[row, 0]
         trs[row] = (shown + pltpu.roll(shown, 4, 0)) * wm[row, 1]
+    g_copy.wait()
     pl.semaphore_wait(barrier, len(partners))
 
     used = []
@@ -159,13 +166,21 @@
             total = term if total is None else total + term
         return total
 
-    def back_rows(cat, layer, p, row, count):
-        total = None
-        for q in range(3):
-            rows = cat[row:row + count, :, q * CH:(q + 1) * CH].reshape(count * COLS, CH)
-            term = nt_dot(rows, w[layer, 2 - p, (2 - q) * CH:(3 - q) * CH, :])
-            total = term if total is None else total + term
-        return total
+    def back_rows(p, row, count):
+        return mm(gcat[row:row + count].reshape(count * COLS, 3 * CH), wt[p])
+
+    lane_of = lax.broadcasted_iota(jnp.int32, (CH, COLS), 1)
+
+    def turn(values):
+        return values.astype(F32).T
+
+    def lane_shifts(turned):
+        earlier = jnp.where(lane_of > 0, pltpu.roll(turned, 1, 1), 0.0)
+        later = jnp.where(lane_of < COLS - 1, pltpu.roll(turned, COLS - 1, 1), 0.0)
+        return [part.astype(BF16) for part in (earlier, turned, later)]
+
+    def put_turned(index, values):
+        at6[index] = jnp.concatenate(lane_shifts(turn(values)), axis=0)
 
     @pl.when(g == 0)
     def _():
@@ -186,9 +201,12 @@
 
     for row in range(2):
         put_cat(gcat, row + 1, g_ref[row].astype(F32))
-    bh[...] = back_rows(gcat, 1, 1, 1, 2)
-    bh[0:COLS] += back_rows(gcat, 1, 2, 2, 1)
-    bh[COLS:] += back_rows(gcat, 1, 0, 1, 1)
+    for p in range(3):
+        for q in range(3):
+            wt[p, q * CH:(q + 1) * CH, :] = w[1, 2 - p, (2 - q) * CH:(3 - q) * CH, :].T
+    bh[...] = back_rows(1, 1, 2)
+    bh[0:COLS] += back_rows(2, 2, 1)
+    bh[COLS:] += back_rows(0, 1, 1)
 
     def layer_input(index):
         values = xp[index] if index in (0, 3) else x_ref[index - 1]
@@ -199,6 +217,7 @@
             total = total * edge[index]
         up[index] = total.astype(BF16)
         put_cat(ucat, index, total)
+        put_turned(index, total)
 
     arrive(t_mid)
     layer_input(1)
@@ -232,8 +251,8 @@
         s_a[...] = up[2:4]
 
     pair_a = send(s_a, r_a, (g, mate))
-    bh[0:COLS] += back_rows(gcat, 1, 0, 0, 1)
-    bh[COLS:] += back_rows(gcat, 1, 2, 3, 1)
+    bh[0:COLS] += back_rows(0, 0, 1)
+    bh[COLS:] += back_rows(2, 3, 1)
 
     zed = ig[...]
     tangent = jnp.tanh(GELU_SCALE * (zed + GELU_CUBIC * zed * zed * zed))
@@ -259,38 +278,19 @@
     f_low = send(fp.at[2], fp.at[0], (g, dn))
     f_top = send(fp.at[1], fp.at[3], (g, up_lat))
 
-    def put_turned(source, places):
-        turned = source.astype(F32).T.astype(BF16)
-
-        @pl.when(g == 1)
-        def _():
-            for block, k in places:
-                at[3 * CH * block:3 * CH * (block + 1), k * COLS:(k + 1) * COLS] = turned
-
-        @pl.when(g == 0)
-        def _():
-            for block, k in places:
-                at[576 * block:576 * (block + 1), k * COLS:(k + 1) * COLS] = turned[192:768]
-                at2[576 * block:576 * (block + 1), k * COLS:(k + 1) * COLS] = turned[384:960]
-
     for row in (1, 2):
         put_cat(hcat, row, hp[row].astype(F32))
 
     arrive(pair_a)
+    for row in range(2):
+        put_turned(4 - 2 * core + row, jnp.where(core == 0, r_a[row], hp[row + 1]))
 
     @pl.when(core == 0)
     def _():
-        put_cat(acat, 0, r_a[0].astype(F32))
-        put_cat(acat, 1, r_a[1].astype(F32))
-        for index in range(6):
-            places = [(p, index - p) for p in range(3) if 0 <= index - p <= 3]
-            put_turned(ucat[index] if index < 4 else acat[index - 4], places)
         b6[0:256] = fp[1:3].reshape(256, CH)
 
     @pl.when(core == 1)
     def _():
-        for row in (1, 2):
-            put_turned(hcat[row], [(0, row + 1)])
         b6[0:256] = r_a[...].reshape(256, CH)
         b6[256:384] = gp[0]
         b6[384:640] = g_ref[...].reshape(256, CH)
@@ -305,8 +305,7 @@
     @pl.when(core == 1)
     def _():
         for row in range(2):
-            put_cat(acat, row, r_b[row].astype(F32))
-            put_turned(acat[row], [(0, row)])
+            put_turned(row, r_b[row])
 
     @pl.when(g == 0)
     def _():
@@ -333,13 +332,13 @@
     ]
 
     def gradient_block(xq):
-        def place(j, rows):
+        def operands(j, rows, shift):
             m = 3 * xq + j
-            start = rows * (m + core * (m % 4 - m))
-            return (
-                pl.ds(pl.multiple_of(start, 16), rows),
-                pl.ds(pl.multiple_of(core * (2 - m // 4) * COLS, 16), 512),
-            )
+            p = m // 4
+            left = pl.ds(pl.multiple_of((m % 4) * rows + shift, 16), rows)
+            lead = (1 - core) * p
+            turned = jnp.concatenate([at6[lead + k, left, :] for k in range(4)], axis=1)
+            return turned, pl.ds(pl.multiple_of(core * (2 - p) * COLS, 16), 512)
 
         def store(lane, made, pieces):
             for src, yq, dst, count in pieces:
@@ -355,16 +354,17 @@
         @pl.when(g == 1)
         def _():
             for j in range(3):
-                left, right = place(j, 288)
-                made = mm(at[left, :], b6[right, :]).astype(BF16)
+                turned, right = operands(j, 288, 0)
+                made = mm(turned, b6[right, :]).astype(BF16)
                 for lane in range(3):
                     store(lane, made[:, 128 * lane:128 * (lane + 1)], atmos_pieces[j])
 
         @pl.when(g == 0)
         def _():
             for j in range(3):
-                left, right = place(j, 144)
-                made = mm(at[left, :], b6[right, 0:256]) + mm(at2[left, :], b6s[right, :])
+                even, right = operands(j, 144, 192)
+                odd, _ = operands(j, 144, 384)
+                made = mm(even, b6[right, 0:256]) + mm(odd, b6s[right, :])
                 made = made.astype(BF16)
                 for lane in range(2):
                     store(lane, made[:, 128 * lane:128 * (lane + 1)], ocean_pieces[j])
@@ -488,58 +488,66 @@
                     def _():
                         copy.wait_send()
 
+    def forward_output():
+        h_low.wait_recv()
+        h_top.wait_recv()
+        put_cat(hcat, 0, hp[0].astype(F32) * has_top)
+        put_cat(hcat, 3, hp[3].astype(F32) * has_low)
+        next_ref[...] = (up[1:3].astype(F32) + conv(hcat, 1).reshape(2, COLS, CH)).astype(BF16)
+
+    def backward_output():
+        f_low.wait_recv()
+        f_top.wait_recv()
+        for row in range(4):
+            values = fp[row].astype(F32)
+            if edge[row] is not None:
+                values = values * edge[row]
+            for q, shifted in enumerate(lane_shifts(turn(values))):
+                ft[q, :, row * COLS:(row + 1) * COLS] = shifted
+        total = None
+        for p in range(3):
+            for q in range(3):
+                term = mm(
+                    w[0, 2 - p, (2 - q) * CH:(3 - q) * CH, :],
+                    ft[q, :, p * COLS:(p + 2) * COLS],
+                )
+                total = term if total is None else total + term
+        ig[...] = g_ref[...].reshape(2 * COLS, CH).astype(F32) + total.T
+        for row in range(2):
+            grad = ig[row * COLS:(row + 1) * COLS, :]
+            high = grad.astype(BF16)
+            low = (grad - high.astype(F32)).astype(BF16)
+            shown = (nt_dot(c16[...], high) + nt_dot(c16[...], low))[0:8] * wm[row, 0]
+            tr2s[row] = shown + pltpu.roll(shown, 4, 0)
+
     gradient_block((x + 2) % 4)
     early[0] = ring_one(0, orders[0][0], part, rec1, 4 * WIN)
     gradient_block((x + 1) % 4)
     gradient_block((x + 3) % 4)
     gradient_block(x)
-    early[1] = ring_one(1, orders[1][0], part, rec1, 4 * WIN)
-    first_two(0)
-    first_two(1)
-    early[2] = ring_one(2, orders[2][0], part, rec1, 4 * WIN)
-
-    arrive(h_low)
-    arrive(h_top)
-    put_cat(hcat, 0, hp[0].astype(F32) * has_top)
-    put_cat(hcat, 3, hp[3].astype(F32) * has_low)
-    next_ref[...] = (up[1:3].astype(F32) + conv(hcat, 1).reshape(2, COLS, CH)).astype(BF16)
-    first_relay(0)
-    first_relay(1)
-    first_two(2)
-
-    for row in (1, 2):
-        put_cat(fcat, row, fp[row].astype(F32))
-    arrive(f_low)
-    arrive(f_top)
-    put_cat(fcat, 0, fp[0].astype(F32) * has_top)
-    put_cat(fcat, 3, fp[3].astype(F32) * has_low)
-    total = g_ref[...].reshape(2 * COLS, CH).astype(F32)
-    for p in range(3):
-        total = total + back_rows(fcat, 0, p, p, 2)
-    ig[...] = total
-
-    for row in range(2):
-        grad = ig[row * COLS:(row + 1) * COLS, :]
-        high = grad.astype(BF16)
-        low = (grad - high.astype(F32)).astype(BF16)
-        shown = (nt_dot(c16[...], high) + nt_dot(c16[...], low))[0:8] * wm[row, 0]
-        tr2s[row] = shown + pltpu.roll(shown, 4, 0)
+
+    for k in (1, 2):
+        early[k] = ring_one(k, orders[k][0], part, rec1, 4 * WIN)
+    for k in range(3):
+        first_two(k)
+
+    forward_output()
+    for k in range(3):
+        first_relay(k)
+
+    backward_output()
     back = send(tr2s, tr2r, (1 - g, lat))
-    first_relay(2)
-    second_start(0)
-    second_start(1)
-    second_relay(0)
-    second_relay(1)
-    second_start(2)
-    third_start(0)
-    third_start(1)
-    second_relay(2)
+    for k in range(3):
+        second_start(k)
+    for k in range(3):
+        second_relay(k)
+    for k in range(3):
+        third_start(k)
     arrive(back)
     for row in range(2):
         left = split_pair(wm[row, 0] * wm[row, 1] * tr2r[row])
         total = ig[row * COLS:(row + 1) * COLS, :] + tn_dot(left, m16[...])
         fgrad_ref[row] = total.astype(BF16)
-    third_start(2)
     assert len(used) <= base
     for k in range(3):
         third_end(k)
@@ -547,13 +555,9 @@
         copy.wait_send()
 
 
-def finish_body(next_in, fgrad_in, grads_in, next_out, fgrad_out, ocean_out, atmos_out, flat, sems):
-    copies = [
-        pltpu.make_async_copy(next_in, next_out.at[0], sems.at[0]),
-        pltpu.make_async_copy(fgrad_in, fgrad_out.at[0], sems.at[1]),
-    ]
-    for copy in copies:
-        copy.start()
+def finish_body(next_in, fgrad_in, grads_in, next_out, fgrad_out, ocean_out, atmos_out, flat):
+    next_out[0] = next_in[...]
+    fgrad_out[0] = fgrad_in[...]
     atmos_factor = 1.0 / math.sqrt(256 * 128)
     for lane in range(3):
         atmos_out[pl.ds(lane, 27, stride=3), :] = grads_in[1, lane, 0:27, :] * atmos_factor
@@ -579,9 +583,6 @@
         after = pltpu.roll(flat[21:42], 96, 1)
         lanes = lax.broadcasted_iota(jnp.int32, (21, 128), 1)
         ocean_out[...] = jnp.where(lanes < 96, here, after)
-
-    for copy in copies:
-        copy.wait()
 
 
 def local(
@@ -608,19 +609,19 @@
             jax.ShapeDtypeStruct((2, COLS, CH), BF16),
             jax.ShapeDtypeStruct((2, 3, 32, 128), F32),
         ),
-        in_specs=[vmem, vmem, hbm, hbm, vmem, vmem, vmem, vmem, vmem],
+        in_specs=[hbm, hbm, hbm, hbm, vmem, vmem, vmem, vmem, vmem],
         out_specs=(vmem, vmem, vmem),
         scratch_shapes=[
-            buf(2, 3, 3 * CH, CH), buf(2, 3, 576, 192),
-            rows4, rows4, rows4, rows4, rows4, cat4, cat4, cat4, cat4,
-            buf(2, COLS, 3 * CH),
+            rows2, rows2, buf(2, 3, 3 * CH, CH), buf(2, 3, 576, 192),
+            rows4, rows4, rows4, rows4, rows4, cat4, cat4, cat4,
+            buf(3, 3 * CH, CH), buf(3, CH, 4 * COLS),
             pltpu.VMEM((8, CH), F32), pltpu.VMEM((8, CH), F32), buf(16, CH), buf(16, CH),
             pltpu.VMEM((2, 2, 8, COLS), F32), small4, small2, small4, small2, small2, wide, wide,
-            rows2, rows2, rows2, rows2, buf(768, CH), buf(768, 256), buf(3456, 512), buf(1728, 512),
+            rows2, rows2, rows2, rows2, buf(768, CH), buf(768, 256), buf(6, 3 * CH, COLS),
             buf(3, 4, 4 * WIN, 128), buf(3, 2, 2 * WIN, 128), buf(3, 2, 4 * WIN, 128),
             buf(3, 4, WIN, 128), buf(3, 2, WIN // 2, 128), buf(3, 2, WIN, 128),
             pltpu.VMEM((240, 128), F32), buf(3, 8, 32, 128), buf(2, 4, 3, 32, 128),
-            pltpu.SemaphoreType.DMA((2,)), pltpu.SemaphoreType.DMA((NSEM,)),
+            pltpu.SemaphoreType.DMA((4,)), pltpu.SemaphoreType.DMA((NSEM,)),
             pltpu.SemaphoreType.DMA((NSEM,)),
         ],
         compiler_params=pltpu.CompilerParams(
@@ -642,9 +643,9 @@
             jax.ShapeDtypeStruct((21, 128), F32),
             jax.ShapeDtypeStruct((81, 128), F32),
         ),
-        in_specs=[hbm, hbm, vmem],
-        out_specs=(hbm, hbm, vmem, vmem),
-        scratch_shapes=[pltpu.VMEM((48, 128), F32), pltpu.SemaphoreType.DMA((2,))],
+        in_specs=[vmem, vmem, vmem],
+        out_specs=(vmem, vmem, vmem, vmem),
+        scratch_shapes=[pltpu.VMEM((48, 128), F32)],
     )(next_field, field_grad, grads)
     return (next_field, field_grad, ocean_rows.reshape(-1)[:2592], atmos_rows.reshape(-1))
 

time: 69.5 us -> 53.7 us (0.77)
  Pallas kernels: 68.6 us -> 52.9 us
    pallas_call x1, Pallas kernels: 14.5 us -> 2.03 us  [local(): pl.pallas_call(finish_body, out_shape=(jax.ShapeDtypeStruct((1, 2, COLS,...]
    pallas_call x1, Pallas kernels: 54 us -> 50.8 us  [local(): pl.pallas_call(body, out_shape=(jax.ShapeDtypeStruct((2, COLS, CH), BF16)...]
where the time goes in v3:
time: 53.7 us; the launch traced here: 53.5 us
  Pallas kernels  52.9 us (99%)
  between operations  0.64 us (1%)
    pallas_call x1, Pallas kernels, local(): pl.pallas_call(body, out_shape=(jax.ShapeDtypeStruct((2, COLS, CH), BF16)...  50.8 us
    pallas_call x1, Pallas kernels, local(): pl.pallas_call(finish_body, out_shape=(jax.ShapeDtypeStruct((1, 2, COLS,...  2.03 us

profile of v3, /device:TPU:1, one launch (start us, length us, event | category | flops | bytes accessed | tf_op | source)
XLA Modules:
  0.0 53.5 jit_solution(14335839792553890575)
XLA Ops:
  0.6 50.8 %shard_map.120 = (bf16[2,128,384]{2,1,0:T(8,128)(2,1)}, bf16[2,128,384]{2,1,0:T(8,128)(2,1)}, f32[2,3,32,128]{3,2,1,0:T(8,128)}) custom-call(bf16[2,128,384]{2,1,0:T(8,128)(2,1)} %bitcast.11, bf16[2,128,384]{2,1,0:T(8,128)(2,1)} %bitcast.12, bf16[2,3,1152,384]{3,2,1,0:T(8,128)(2,1)} %bitcast.9, bf16[2,3,576,192]{3,2,1,0:T(8,128)(2,1)} %bitcast.10, ...), custom_call_target="tpu_custom_call" | custom-call | flops 4100000000 | bytes 8000000 | tf_op jit(solution)/shard_map/pallas_call | solution.py:605
  51.5 2.0 %shard_map.121 = (bf16[1,2,128,384]{3,2,1,0:T(8,128)(2,1)}, bf16[1,2,128,384]{3,2,1,0:T(8,128)(2,1)}, f32[21,128]{1,0:T(8,128)}, f32[81,128]{1,0:T(8,128)}) custom-call(bf16[2,128,384]{2,1,0:T(8,128)(2,1)} %get-tuple-element.11.next_in, bf16[2,128,384]{2,1,0:T(8,128)(2,1)} %get-tuple-element.12.fgrad_in, f32[2,3,32,128]{3,2,1,0:T(8,128)} %get-tuple-element.13.grads_in), custom_call_target="tpu_custom_call" | custom-call | tf_op jit(solution)/shard_map/pallas_call | solution.py:638

commit v4 on v3

--- a/solution.py
+++ b/solution.py
@@ -36,12 +36,12 @@
 
 
 def body(
-    x_hbm, g_hbm, ak_ref, ok_ref, os_ref, oc_ref, af_ref, ac_ref, wet_ref,
-    next_ref, fgrad_ref, grads_ref,
-    x_ref, g_ref, w, okv, xp, gp, hp, fp, up, gcat, ucat, hcat,
+    x_hbm, g_hbm, ak_ref, ok_ref, os_hbm, oc_hbm, af_hbm, ac_hbm, wet_hbm,
+    next_hbm, fgrad_hbm, grads_ref,
+    os_ref, oc_ref, af_ref, ac_ref, wet_ref, next_ref, fgrad_ref, x_ref, g_ref, w, okv, xp, gp, hp, fp, up, gcat, ucat, hcat,
     wt, ft, m8, c8, m16, c16, wm, wmp, trs, trp, tr2s, tr2r, bh, ig,
     s_a, r_a, s_b, r_b, b6, b6s, at6,
-    part, rec1, rec2, part2, rec3, rec4, dsum, zsend, zrec,
+    part, rec1, rec2, part2, rec5, rec4, dsum, zsend, zrec,
     wsem, ssem, rsem,
 ):
     g = lax.axis_index("grp")
@@ -58,6 +58,7 @@
     up_lat = (lat + 127) % 128
     x_plus, x_minus = spot((x + 1) % 4, y, z, core), spot((x + 3) % 4, y, z, core)
     y_plus, y_minus = spot(x, (y + 1) % 4, z, core), spot(x, (y + 3) % 4, z, core)
+    x_far, y_far = spot((x + 2) % 4, y, z, core), spot(x, (y + 2) % 4, z, core)
     mate = lat + 1 - 2 * core
     has_top = jnp.where(lat > 0, 1.0, 0.0).astype(F32)
     has_low = jnp.where(lat < 127, 1.0, 0.0).astype(F32)
@@ -65,12 +66,19 @@
 
     x_copy = pltpu.make_async_copy(x_hbm, x_ref, wsem.at[2])
     g_copy = pltpu.make_async_copy(g_hbm, g_ref, wsem.at[3])
-    x_copy.start()
-    g_copy.start()
+    maps = [
+        pltpu.make_async_copy(src, dst, wsem.at[4 + index])
+        for index, (src, dst) in enumerate((
+            (os_hbm, os_ref), (oc_hbm, oc_ref), (af_hbm, af_ref), (ac_hbm, ac_ref),
+            (wet_hbm, wet_ref),
+        ))
+    ]
+    for copy in (*maps, x_copy, g_copy):
+        copy.start()
 
     barrier = pltpu.get_barrier_semaphore()
     partners = [(g, dn), (g, up_lat), (1 - g, dn), (1 - g, up_lat)]
-    partners += [(g, other) for other in (x_plus, x_minus, y_plus, y_minus)]
+    partners += [(g, other) for other in (x_plus, x_minus, x_far, y_plus, y_minus, y_far)]
     for step in range(16):
         if step > 0:
             hop = (step // 2) % 4
@@ -96,6 +104,8 @@
     lane_id = lax.broadcasted_iota(jnp.int32, (half, CH), 1)
     lower = jnp.where(row_id == lane_id, 1.0, 0.0).astype(BF16)
     upper = jnp.where(row_id + half == lane_id, 1.0, 0.0).astype(BF16)
+    for copy in maps:
+        copy.wait()
     is_atmos = g.astype(F32)
     is_ocean = 1.0 - is_atmos
     for dst, ocean, atmos in ((m8, os_ref, af_ref), (c8, oc_ref, ac_ref)):
@@ -232,6 +242,14 @@
     ig[0:COLS] += mm(ucat[0], w[0, 0])
     ig[COLS:] += mm(ucat[3], w[0, 2])
 
+    zed = ig[...]
+    tangent = jnp.tanh(GELU_SCALE * (zed + GELU_CUBIC * zed * zed * zed))
+    hidden = (0.5 * zed * (1.0 + tangent)).astype(BF16).reshape(2, COLS, CH)
+    hp[1:3] = hidden
+    ig[...] = 0.5 * (1.0 + tangent) + 0.5 * zed * (1.0 - tangent * tangent) * GELU_SCALE * (
+        1.0 + 3.0 * GELU_CUBIC * zed * zed
+    )
+
     arrive(g_low)
     arrive(g_top)
     top_values = gp[0].astype(F32) * has_top
@@ -254,14 +272,7 @@
     bh[0:COLS] += back_rows(0, 0, 1)
     bh[COLS:] += back_rows(2, 3, 1)
 
-    zed = ig[...]
-    tangent = jnp.tanh(GELU_SCALE * (zed + GELU_CUBIC * zed * zed * zed))
-    hidden = (0.5 * zed * (1.0 + tangent)).astype(BF16).reshape(2, COLS, CH)
-    slope = 0.5 * (1.0 + tangent) + 0.5 * zed * (1.0 - tangent * tangent) * GELU_SCALE * (
-        1.0 + 3.0 * GELU_CUBIC * zed * zed
-    )
-    first_grad = (bh[...] * slope).astype(BF16).reshape(2, COLS, CH)
-    hp[1:3] = hidden
+    first_grad = (bh[...] * ig[...]).astype(BF16).reshape(2, COLS, CH)
     fp[1:3] = first_grad
 
     @pl.when(core == 0)
@@ -278,9 +289,6 @@
     f_low = send(fp.at[2], fp.at[0], (g, dn))
     f_top = send(fp.at[1], fp.at[3], (g, up_lat))
 
-    for row in (1, 2):
-        put_cat(hcat, row, hp[row].astype(F32))
-
     arrive(pair_a)
     for row in range(2):
         put_turned(4 - 2 * core + row, jnp.where(core == 0, r_a[row], hp[row + 1]))
@@ -315,7 +323,7 @@
         b6s[...] = mm(b6[...], swap).astype(BF16)
 
 
-    ids_x, ids_y = (x, x_plus, x_minus), (y, y_plus, y_minus)
+    ids_x, ids_y = (x, x_plus, x_minus, x_far), (y, y_plus, y_minus, y_far)
     mixed_a = tuple(a + core * (b - a) for a, b in zip(ids_x, ids_y))
     mixed_b = tuple(b + core * (a - b) for a, b in zip(ids_x, ids_y))
     orders = [(ids_x, ids_y), (ids_y, ids_x), (mixed_a, mixed_b)]
@@ -373,7 +381,7 @@
         return pl.ds(0, rows // 2), pl.ds(rows // 2, rows // 2)
 
     def ring_one(lane, ids, source, near, rows):
-        me, plus, minus = ids
+        me, plus, minus, far_id = ids
         low, high = parts_of(rows)
         across = (me + 2) % 4
         one_p = send(source.at[lane, across, low], near.at[lane, 0], (g, plus))
@@ -381,14 +389,22 @@
         return one_p, one_m
 
     def ring_two(lane, ids, source, far, rows, plus_side):
-        me, plus, minus = ids
+        me, plus, minus, far_id = ids
         low, high = parts_of(rows)
         if plus_side:
             return send(source.at[lane, (me + 1) % 4, high], far.at[lane, 0, high], (g, plus))
         return send(source.at[lane, (me + 3) % 4, low], far.at[lane, 1, low], (g, minus))
 
+    def direct(lane, ids, source, far, wide, rows):
+        me, plus, minus, far_id = ids
+        return (
+            send(source.at[lane, (me + 2) % 4], wide.at[lane], (g, far_id)),
+            send(source.at[lane, (me + 1) % 4], far.at[lane, 0], (g, plus)),
+            send(source.at[lane, (me + 3) % 4], far.at[lane, 1], (g, minus)),
+        )
+
     def ring_relay(lane, ids, source, near, far, rows, early):
-        me, plus, minus = ids
+        me, plus, minus, far_id = ids
         low, high = parts_of(rows)
         ahead, behind = (me + 1) % 4, (me + 3) % 4
         arrive(early[0])
@@ -423,13 +439,7 @@
     def second_start(k):
         made = ring_sum(k, orders[k][0], part, rec2, middle[k] + late[k])
         part2[k] = made.astype(BF16).reshape(4, WIN, 128)
-        early2[k] = ring_one(k, orders[k][1], part2, rec3, WIN)
-        middle2[k] = tuple(
-            ring_two(k, orders[k][1], part2, rec4, WIN, side) for side in (True, False)
-        )
-
-    def second_relay(k):
-        late2[k] = ring_relay(k, orders[k][1], part2, rec3, rec4, WIN, early2[k])
+        late2[k] = direct(k, orders[k][1], part2, rec4, rec5, WIN)
 
     base = 56
 
@@ -442,7 +452,7 @@
         )
 
     def third_start(k):
-        dsum[0:WIN] = ring_sum(k, orders[k][1], part2, rec4, middle2[k] + late2[k])
+        dsum[0:WIN] = ring_sum(k, orders[k][1], part2, rec4, late2[k]) + rec5[k].astype(F32)
         dsum[WIN:WIN + 16] = jnp.zeros((16, 128), F32)
         for hop in (2, 1, 3, 0):
             zz = (z + hop) % 4
@@ -489,6 +499,8 @@
                         copy.wait_send()
 
     def forward_output():
+        for row in (1, 2):
+            put_cat(hcat, row, hp[row].astype(F32))
         h_low.wait_recv()
         h_top.wait_recv()
         put_cat(hcat, 0, hp[0].astype(F32) * has_top)
@@ -532,6 +544,8 @@
         first_two(k)
 
     forward_output()
+    next_copy = pltpu.make_async_copy(next_ref, next_hbm, wsem.at[2])
+    next_copy.start()
     for k in range(3):
         first_relay(k)
 
@@ -539,8 +553,6 @@
     back = send(tr2s, tr2r, (1 - g, lat))
     for k in range(3):
         second_start(k)
-    for k in range(3):
-        second_relay(k)
     for k in range(3):
         third_start(k)
     arrive(back)
@@ -548,9 +560,13 @@
         left = split_pair(wm[row, 0] * wm[row, 1] * tr2r[row])
         total = ig[row * COLS:(row + 1) * COLS, :] + tn_dot(left, m16[...])
         fgrad_ref[row] = total.astype(BF16)
+    fgrad_copy = pltpu.make_async_copy(fgrad_ref, fgrad_hbm, wsem.at[3])
+    fgrad_copy.start()
     assert len(used) <= base
     for k in range(3):
         third_end(k)
+    next_copy.wait()
+    fgrad_copy.wait()
     for copy in used:
         copy.wait_send()
 
@@ -609,19 +625,20 @@
             jax.ShapeDtypeStruct((2, COLS, CH), BF16),
             jax.ShapeDtypeStruct((2, 3, 32, 128), F32),
         ),
-        in_specs=[hbm, hbm, hbm, hbm, vmem, vmem, vmem, vmem, vmem],
-        out_specs=(vmem, vmem, vmem),
+        in_specs=[hbm] * 9,
+        out_specs=(hbm, hbm, vmem),
         scratch_shapes=[
-            rows2, rows2, buf(2, 3, 3 * CH, CH), buf(2, 3, 576, 192),
+            buf(4, 192), buf(4, 192), buf(4, CH), buf(4, CH), pltpu.VMEM((2, 256), jnp.int32),
+            rows2, rows2, rows2, rows2, buf(2, 3, 3 * CH, CH), buf(2, 3, 576, 192),
             rows4, rows4, rows4, rows4, rows4, cat4, cat4, cat4,
             buf(3, 3 * CH, CH), buf(3, CH, 4 * COLS),
             pltpu.VMEM((8, CH), F32), pltpu.VMEM((8, CH), F32), buf(16, CH), buf(16, CH),
             pltpu.VMEM((2, 2, 8, COLS), F32), small4, small2, small4, small2, small2, wide, wide,
             rows2, rows2, rows2, rows2, buf(768, CH), buf(768, 256), buf(6, 3 * CH, COLS),
             buf(3, 4, 4 * WIN, 128), buf(3, 2, 2 * WIN, 128), buf(3, 2, 4 * WIN, 128),
-            buf(3, 4, WIN, 128), buf(3, 2, WIN // 2, 128), buf(3, 2, WIN, 128),
+            buf(3, 4, WIN, 128), buf(3, WIN, 128), buf(3, 2, WIN, 128),
             pltpu.VMEM((240, 128), F32), buf(3, 8, 32, 128), buf(2, 4, 3, 32, 128),
-            pltpu.SemaphoreType.DMA((4,)), pltpu.SemaphoreType.DMA((NSEM,)),
+            pltpu.SemaphoreType.DMA((9,)), pltpu.SemaphoreType.DMA((NSEM,)),
             pltpu.SemaphoreType.DMA((NSEM,)),
         ],
         compiler_params=pltpu.CompilerParams(

time: 53.7 us -> 51.6 us (0.961)
  Pallas kernels: 52.9 us -> 50.8 us
    pallas_call x1, Pallas kernels: 50.8 us -> 48.8 us  [local(): pl.pallas_call(body, out_shape=(jax.ShapeDtypeStruct((2, COLS, CH), BF16)...]
where the time goes in v4:
time: 51.6 us; the launch traced here: 51.5 us
  Pallas kernels  50.8 us (98%)
  between operations  0.64 us (1%)
    pallas_call x1, Pallas kernels, local(): pl.pallas_call(body, out_shape=(jax.ShapeDtypeStruct((2, COLS, CH), BF16)...  48.8 us
    pallas_call x1, Pallas kernels, local(): pl.pallas_call(finish_body, out_shape=(jax.ShapeDtypeStruct((1, 2, COLS,...  2.03 us

profile of v4, /device:TPU:1, one launch (start us, length us, event | category | flops | bytes accessed | tf_op | source)
XLA Modules:
  0.0 51.5 jit_solution(195928363291873969)
XLA Ops:
  0.6 48.8 %shard_map.120 = (bf16[2,128,384]{2,1,0:T(8,128)(2,1)}, bf16[2,128,384]{2,1,0:T(8,128)(2,1)}, f32[2,3,32,128]{3,2,1,0:T(8,128)}) custom-call(bf16[2,128,384]{2,1,0:T(8,128)(2,1)} %bitcast.11, bf16[2,128,384]{2,1,0:T(8,128)(2,1)} %bitcast.12, bf16[2,3,1152,384]{3,2,1,0:T(8,128)(2,1)} %bitcast.9, bf16[2,3,576,192]{3,2,1,0:T(8,128)(2,1)} %bitcast.10, ...), custom_call_target="tpu_custom_call" | custom-call | flops 4100000000 | bytes 8000000 | tf_op jit(solution)/shard_map/pallas_call | solution.py:621
  49.4 2.0 %shard_map.121 = (bf16[1,2,128,384]{3,2,1,0:T(8,128)(2,1)}, bf16[1,2,128,384]{3,2,1,0:T(8,128)(2,1)}, f32[21,128]{1,0:T(8,128)}, f32[81,128]{1,0:T(8,128)}) custom-call(bf16[2,128,384]{2,1,0:T(8,128)(2,1)} %get-tuple-element.11.next_in, bf16[2,128,384]{2,1,0:T(8,128)(2,1)} %get-tuple-element.12.fgrad_in, f32[2,3,32,128]{3,2,1,0:T(8,128)} %get-tuple-element.13.grads_in), custom_call_target="tpu_custom_call" | custom-call | tf_op jit(solution)/shard_map/pallas_call | solution.py:655

commit v5 on v4

--- a/solution.py
+++ b/solution.py
@@ -37,8 +37,8 @@
 
 def body(
     x_hbm, g_hbm, ak_ref, ok_ref, os_hbm, oc_hbm, af_hbm, ac_hbm, wet_hbm,
-    next_hbm, fgrad_hbm, grads_ref,
-    os_ref, oc_ref, af_ref, ac_ref, wet_ref, next_ref, fgrad_ref, x_ref, g_ref, w, okv, xp, gp, hp, fp, up, gcat, ucat, hcat,
+    next_ref, fgrad_ref, grads_ref,
+    os_ref, oc_ref, af_ref, ac_ref, wet_ref, x_ref, g_ref, w, okv, xp, gp, hp, fp, up, gcat, ucat, hcat,
     wt, ft, m8, c8, m16, c16, wm, wmp, trs, trp, tr2s, tr2r, bh, ig,
     s_a, r_a, s_b, r_b, b6, b6s, at6,
     part, rec1, rec2, part2, rec5, rec4, dsum, zsend, zrec,
@@ -451,22 +451,25 @@
             device_id=device, device_id_type=MESH,
         )
 
+    def z_used(k, hop, cc):
+        used_here = (g == 1) if k == 2 else (g >= 0)
+        if hop == 0:
+            used_here = used_here & ((core != g) | (core != cc))
+        return used_here
+
     def third_start(k):
         dsum[0:WIN] = ring_sum(k, orders[k][1], part2, rec4, late2[k]) + rec5[k].astype(F32)
         dsum[WIN:WIN + 16] = jnp.zeros((16, 128), F32)
-        for hop in (2, 1, 3, 0):
+        for hop in (0, 1, 3, 2):
             zz = (z + hop) % 4
             place = g * (8 * (y % 2) + 54 * zz) + (1 - g) * ((12 * y) % 16 + 27 * zz)
             for cc in range(2):
                 slot = 2 * hop + cc
                 zsend[k, slot] = dsum[pl.ds(place + 27 * cc * g, 32), :].astype(BF16)
-                copy = z_copy(k, slot, g, (4 - hop) % 4, (core, spot(x, y, zz, cc)))
-                if hop > 0:
-                    copy.start()
-                else:
-                    @pl.when((core != g) | (core != cc))
-                    def _():
-                        copy.start()
+
+                @pl.when(z_used(k, hop, cc))
+                def _():
+                    z_copy(k, slot, g, (4 - hop) % 4, (core, spot(x, y, zz, cc))).start()
 
     def third_end(k):
         @pl.when(core == g)
@@ -474,6 +477,8 @@
             zrec[g, 0, k] = zsend[k, core]
 
         for comp in range(2):
+            if comp == 0 and k == 2:
+                continue
             for source in range(4):
                 copy = z_copy(k, 0, comp, source, (g, mate))
                 if source > 0:
@@ -490,13 +495,10 @@
         for hop in range(4):
             for cc in range(2):
                 slot = 2 * hop + cc
-                copy = z_copy(k, slot, g, 0, (g, mate))
-                if hop > 0:
-                    copy.wait_send()
-                else:
-                    @pl.when((core != g) | (core != cc))
-                    def _():
-                        copy.wait_send()
+
+                @pl.when(z_used(k, hop, cc))
+                def _():
+                    z_copy(k, slot, g, 0, (g, mate)).wait_send()
 
     def forward_output():
         for row in (1, 2):
@@ -544,8 +546,6 @@
         first_two(k)
 
     forward_output()
-    next_copy = pltpu.make_async_copy(next_ref, next_hbm, wsem.at[2])
-    next_copy.start()
     for k in range(3):
         first_relay(k)
 
@@ -560,13 +560,9 @@
         left = split_pair(wm[row, 0] * wm[row, 1] * tr2r[row])
         total = ig[row * COLS:(row + 1) * COLS, :] + tn_dot(left, m16[...])
         fgrad_ref[row] = total.astype(BF16)
-    fgrad_copy = pltpu.make_async_copy(fgrad_ref, fgrad_hbm, wsem.at[3])
-    fgrad_copy.start()
     assert len(used) <= base
     for k in range(3):
         third_end(k)
-    next_copy.wait()
-    fgrad_copy.wait()
     for copy in used:
         copy.wait_send()
 
@@ -621,15 +617,15 @@
     next_field, field_grad, grads = pl.pallas_call(
         body,
         out_shape=(
-            jax.ShapeDtypeStruct((2, COLS, CH), BF16),
-            jax.ShapeDtypeStruct((2, COLS, CH), BF16),
-            jax.ShapeDtypeStruct((2, 3, 32, 128), F32),
+            pltpu.VMEM((2, COLS, CH), BF16),
+            pltpu.VMEM((2, COLS, CH), BF16),
+            pltpu.VMEM((2, 3, 32, 128), F32),
         ),
         in_specs=[hbm] * 9,
-        out_specs=(hbm, hbm, vmem),
+        out_specs=(vmem, vmem, vmem),
         scratch_shapes=[
             buf(4, 192), buf(4, 192), buf(4, CH), buf(4, CH), pltpu.VMEM((2, 256), jnp.int32),
-            rows2, rows2, rows2, rows2, buf(2, 3, 3 * CH, CH), buf(2, 3, 576, 192),
+            rows2, rows2, buf(2, 3, 3 * CH, CH), buf(2, 3, 576, 192),
             rows4, rows4, rows4, rows4, rows4, cat4, cat4, cat4,
             buf(3, 3 * CH, CH), buf(3, CH, 4 * COLS),
             pltpu.VMEM((8, CH), F32), pltpu.VMEM((8, CH), F32), buf(16, CH), buf(16, CH),
@@ -663,6 +659,7 @@
         in_specs=[vmem, vmem, vmem],
         out_specs=(vmem, vmem, vmem, vmem),
         scratch_shapes=[pltpu.VMEM((48, 128), F32)],
+        compiler_params=pltpu.CompilerParams(vmem_limit_bytes=4 * 1024 * 1024),
     )(next_field, field_grad, grads)
     return (next_field, field_grad, ocean_rows.reshape(-1)[:2592], atmos_rows.reshape(-1))
 

time: 51.6 us -> 49.4 us (0.957)
  Pallas kernels: 50.8 us -> 48.7 us
    pallas_call x1, Pallas kernels: 2.03 us -> 0.9 us  [local(): pl.pallas_call(finish_body, out_shape=(jax.ShapeDtypeStruct((1, 2, COLS,...]
    pallas_call x1, Pallas kernels: 48.8 us -> 47.8 us  [local(): pl.pallas_call(body, out_shape=(pltpu.VMEM((2, COLS, CH), BF16), pltpu.VM...]
where the time goes in v5:
time: 49.4 us; the launch traced here: 49.3 us
  Pallas kernels  48.7 us (99%)
  between operations  0.64 us (1%)
    pallas_call x1, Pallas kernels, local(): pl.pallas_call(body, out_shape=(pltpu.VMEM((2, COLS, CH), BF16), pltpu.VM...  47.8 us

profile of v5, /device:TPU:1, one launch (start us, length us, event | category | flops | bytes accessed | tf_op | source)
XLA Modules:
  0.0 49.3 jit_solution(12621659187566650049)
XLA Ops:
  0.6 47.8 %shard_map.120 = (bf16[2,128,384]{2,1,0:T(8,128)(2,1)S(1)}, bf16[2,128,384]{2,1,0:T(8,128)(2,1)S(1)}, f32[2,3,32,128]{3,2,1,0:T(8,128)S(1)}) custom-call(bf16[2,128,384]{2,1,0:T(8,128)(2,1)} %bitcast.11, bf16[2,128,384]{2,1,0:T(8,128)(2,1)} %bitcast.12, bf16[2,3,1152,384]{3,2,1,0:T(8,128)(2,1)} %bitcast.9, bf16[2,3,576,192]{3,2,1,0:T(8,128)(2,1)} %bitcast.10, ...), custom_call_target="tpu_custom_call" | custom-call | flops 4100000000 | bytes 8000000 | tf_op jit(solution)/shard_map/pallas_call | solution.py:617
  48.4 0.9 %shard_map.121 = (bf16[1,2,128,384]{3,2,1,0:T(8,128)(2,1)}, bf16[1,2,128,384]{3,2,1,0:T(8,128)(2,1)}, f32[21,128]{1,0:T(8,128)}, f32[81,128]{1,0:T(8,128)}) custom-call(bf16[2,128,384]{2,1,0:T(8,128)(2,1)S(1)} %get-tuple-element.11.next_in, bf16[2,128,384]{2,1,0:T(8,128)(2,1)S(1)} %get-tuple-element.12.fgrad_in, f32[2,3,32,128]{3,2,1,0:T(8,128)S(1)} %get-tuple-element.13.grads_in), custom_call_target="tpu_custom_call" | custom-call | tf_op jit(solution)/shard_map/pallas_call | solution.py:651

commit v6 on v5

--- a/solution.py
+++ b/solution.py
@@ -567,12 +567,13 @@
         copy.wait_send()
 
 
-def finish_body(next_in, fgrad_in, grads_in, next_out, fgrad_out, ocean_out, atmos_out, flat):
+def finish_body(next_in, fgrad_in, grads_in, next_out, fgrad_out, ocean_out, atmos_out, flat, spread):
     next_out[0] = next_in[...]
     fgrad_out[0] = fgrad_in[...]
     atmos_factor = 1.0 / math.sqrt(256 * 128)
     for lane in range(3):
-        atmos_out[pl.ds(lane, 27, stride=3), :] = grads_in[1, lane, 0:27, :] * atmos_factor
+        spread[pl.ds(lane, 32, stride=3), :] = grads_in[1, lane] * atmos_factor
+    atmos_out[...] = spread[0:81]
     left = lax.broadcasted_iota(jnp.int32, (14, 128), 1) < 64
 
     def rows(lane, start):
@@ -658,7 +659,7 @@
         ),
         in_specs=[vmem, vmem, vmem],
         out_specs=(vmem, vmem, vmem, vmem),
-        scratch_shapes=[pltpu.VMEM((48, 128), F32)],
+        scratch_shapes=[pltpu.VMEM((56, 128), F32), pltpu.VMEM((104, 128), F32)],
         compiler_params=pltpu.CompilerParams(vmem_limit_bytes=4 * 1024 * 1024),
     )(next_field, field_grad, grads)
     return (next_field, field_grad, ocean_rows.reshape(-1)[:2592], atmos_rows.reshape(-1))

time: 49.4 us -> 49.4 us (level)
  no operation moved by 1% of the time
where the time goes in v6:
time: 49.4 us; the launch traced here: 49.3 us
  Pallas kernels  48.7 us (99%)
  between operations  0.64 us (1%)
    pallas_call x1, Pallas kernels, local(): pl.pallas_call(body, out_shape=(pltpu.VMEM((2, COLS, CH), BF16), pltpu.VM...  47.8 us

profile of v6, /device:TPU:1, one launch (start us, length us, event | category | flops | bytes accessed | tf_op | source)
XLA Modules:
  0.0 49.3 jit_solution(5909545368478008896)
XLA Ops:
  0.6 47.8 %shard_map.120 = (bf16[2,128,384]{2,1,0:T(8,128)(2,1)S(1)}, bf16[2,128,384]{2,1,0:T(8,128)(2,1)S(1)}, f32[2,3,32,128]{3,2,1,0:T(8,128)S(1)}) custom-call(bf16[2,128,384]{2,1,0:T(8,128)(2,1)} %bitcast.11, bf16[2,128,384]{2,1,0:T(8,128)(2,1)} %bitcast.12, bf16[2,3,1152,384]{3,2,1,0:T(8,128)(2,1)} %bitcast.9, bf16[2,3,576,192]{3,2,1,0:T(8,128)(2,1)} %bitcast.10, ...), custom_call_target="tpu_custom_call" | custom-call | flops 4100000000 | bytes 8000000 | tf_op jit(solution)/shard_map/pallas_call | solution.py:618
  48.4 0.9 %shard_map.121 = (bf16[1,2,128,384]{3,2,1,0:T(8,128)(2,1)}, bf16[1,2,128,384]{3,2,1,0:T(8,128)(2,1)}, f32[21,128]{1,0:T(8,128)}, f32[81,128]{1,0:T(8,128)}) custom-call(bf16[2,128,384]{2,1,0:T(8,128)(2,1)S(1)} %get-tuple-element.11.next_in, bf16[2,128,384]{2,1,0:T(8,128)(2,1)S(1)} %get-tuple-element.12.fgrad_in, f32[2,3,32,128]{3,2,1,0:T(8,128)S(1)} %get-tuple-element.13.grads_in), custom_call_target="tpu_custom_call" | custom-call | tf_op jit(solution)/shard_map/pallas_call | solution.py:652
